TPU v7x, 32 devices: a whole 2x2x4 slice. The times are simulated.
32 devices in a mesh: grp: 8 (over z, core), voc: 4 (over y, x).
Axes of the slice: x: 2, y: 2, z: 4, core: 2. Of those that a mesh axis runs over, the one named last changes fastest.
Arguments:
- student_hidden: bfloat16 [192, 4096], P('grp', 'voc')
- norm_gain: float32 [4096], P('voc'), may hold values from 0.5 to 1.5
- teacher_hidden: bfloat16 [192, 5120], P('grp', 'voc')
- student_head: bfloat16 [4096, 12288], P(None, ('grp', 'voc'))
- teacher_head: bfloat16 [5120, 12288], P(None, ('grp', 'voc'))
- episode_source: int32 [96], replicated, may hold values from 0 to 95, as said below
- lengths: int32 [96], replicated, may hold values from 1 to 2, 120 in all
Outputs:
- loss: float32 [], replicated
- grad_hidden: bfloat16 [192, 4096], P('grp', 'voc')
- grad_gain: float32 [4096], P('voc')
- grad_head: bfloat16 [4096, 12288], P(None, ('grp', 'voc'))
Inputs may be any that keep to these rules, and one draw needn't show every extreme that they name: `episode_source`: A permutation of the episodes. Student episodes 12 * s to 12 * s + 11 form group s, teacher episodes likewise form teacher group t; at most 2 episodes of one student group come from one teacher group, and that many in some pair.
All inputs are finite; a program needn't handle non-finite values.
Results may differ from a plain program's by a relative error of at most 0.04.
Values may be sent and summed in bfloat16 or wider, within the bound.
A program may use at most 64 MiB of HBM per device.

v0:
```python
import jax
import jax.numpy as jnp
from jax import lax
from jax.sharding import PartitionSpec as P

DS = 4096
SEQ = 2
MOST = 2


EPSILON = 1e-06


def realign(teacher_hidden, table, group_index, per_group):
    groups = table.shape[0]
    source_group = table // per_group
    source_local = table % per_group
    mine = (source_group == group_index).astype(jnp.int32)
    earlier = jnp.cumsum(mine, axis=1) - mine
    slot_ids = jnp.arange(MOST, dtype=jnp.int32)
    matches = mine[:, :, None] * (earlier[:, :, None] == slot_ids[None, None, :]).astype(jnp.int32)
    send_index = jnp.sum(matches * source_local[:, :, None], axis=1)
    features = teacher_hidden.shape[1]
    episodes = teacher_hidden.reshape(per_group, SEQ, features)
    outgoing = jnp.take(episodes, send_index, axis=0)
    incoming = lax.all_to_all(outgoing, "grp", split_axis=0, concat_axis=0, tiled=True)
    own_groups = lax.dynamic_index_in_dim(source_group, group_index, 0, keepdims=False)
    matching = (own_groups[:, None] == own_groups[None, :]).astype(jnp.int32)
    position = jnp.sum(jnp.tril(matching, -1), axis=1)
    flat_index = own_groups * MOST + position
    received = incoming.reshape(groups * MOST, SEQ, features)
    return jnp.take(received, flat_index, axis=0).reshape(per_group * SEQ, features)


def local(
    student_hidden, norm_gain, teacher_hidden, student_head, teacher_head, episode_source, lengths
):
    groups = lax.axis_size("grp")
    group_index = lax.axis_index("grp")
    rows_group = student_hidden.shape[0]
    per_group = rows_group // SEQ
    hidden_f32 = student_hidden.astype(jnp.float32)
    squares = lax.psum(jnp.sum(hidden_f32 * hidden_f32, axis=1), "voc")
    inverse_rms = lax.rsqrt(squares / DS + EPSILON)
    normed = (hidden_f32 * inverse_rms[:, None] * norm_gain[None, :]).astype(jnp.bfloat16)
    table = episode_source.reshape(groups, per_group)
    aligned = realign(teacher_hidden, table, group_index, per_group)
    teacher_rows, student_rows = (
        lax.all_gather(aligned, "voc", axis=1, tiled=True),
        lax.all_gather(normed, "voc", axis=1, tiled=True),
    )
    teacher_logits = jnp.dot(
        lax.all_gather(teacher_rows, "grp", axis=0, tiled=True),
        teacher_head,
        preferred_element_type=jnp.float32,
    )
    positions = jnp.arange(SEQ, dtype=jnp.int32)
    all_rows = lax.all_gather(student_rows, "grp", axis=0, tiled=True)
    student_logits = jnp.dot(all_rows, student_head, preferred_element_type=jnp.float32)
    lengths_f32 = lengths.astype(jnp.float32)
    valid = positions[None, :] < lengths[:, None]
    token_weight = jnp.where(
        valid, 1.0 / lengths_f32[:, None], jnp.zeros_like(lengths_f32)[:, None]
    ).reshape(-1)
    top_student, top_teacher = lax.pmax(
        (jnp.max(student_logits, axis=1), jnp.max(teacher_logits, axis=1)), ("grp", "voc")
    )
    exp_student = jnp.exp(student_logits - top_student[:, None])
    exp_teacher = jnp.exp(teacher_logits - top_teacher[:, None])
    total_student, total_teacher = lax.psum(
        (jnp.sum(exp_student, axis=1), jnp.sum(exp_teacher, axis=1)), ("grp", "voc")
    )
    log_student = student_logits - (top_student + jnp.log(total_student))[:, None]
    log_teacher = teacher_logits - (top_teacher + jnp.log(total_teacher))[:, None]
    prob_student = jnp.exp(log_student)
    log_ratio = log_student - log_teacher
    divergence = lax.psum(jnp.sum(prob_student * log_ratio, axis=1), ("grp", "voc"))
    loss = jnp.sum(token_weight * divergence)
    logit_grad = (token_weight[:, None] * prob_student * (log_ratio - divergence[:, None])).astype(
        jnp.bfloat16
    )
    grad_head = lax.dot_general(
        all_rows, logit_grad, (((0,), (0,)), ((), ())), preferred_element_type=jnp.float32
    ).astype(jnp.bfloat16)
    full_term = lax.dot_general(
        logit_grad, student_head, (((1,), (1,)), ((), ())), preferred_element_type=jnp.float32
    )
    feature_part = lax.psum_scatter(
        full_term.astype(jnp.bfloat16), "voc", scatter_dimension=1, tiled=True
    )
    normed_grad = lax.psum_scatter(feature_part, "grp", scatter_dimension=0, tiled=True).astype(
        jnp.float32
    )
    scaled = normed_grad * norm_gain[None, :]
    inner = lax.psum(jnp.sum(scaled * hidden_f32, axis=1), "voc")
    grad_hidden = (
        inverse_rms[:, None] * scaled - hidden_f32 * (inverse_rms**3)[:, None] * inner[:, None] / DS
    )
    grad_gain = lax.psum(jnp.sum(normed_grad * hidden_f32 * inverse_rms[:, None], axis=0), "grp")
    return (loss, grad_hidden.astype(jnp.bfloat16), grad_gain, grad_head)


def solution(mesh):
    placed = (
        P("grp", "voc"),
        P("voc"),
        P("grp", "voc"),
        P(None, ("grp", "voc")),
        P(None, ("grp", "voc")),
        P(),
        P(),
    )
    return jax.shard_map(
        local,
        mesh=mesh,
        in_specs=placed,
        out_specs=(P(), P("grp", "voc"), P("voc"), P(None, ("grp", "voc"))),
        check_vma=False,
    )
```

profile of v0, /device:TPU:0, one launch (start us, length us, event | category | flops | bytes accessed | tf_op | source)
XLA Modules:
  0.0 311.5 jit_solution(17097529933251901838)
XLA Ops:
  7.2 1.1 fusion.3
  8.3 11.4 %psum.42 = f32[24]{0:T(128)S(1)} all-reduce(f32[24]{0:T(128)S(1)} %fusion.3), channel_id=1, replica_groups=mesh['grp'=8,'voc'=4] {'voc'}, use_global_device_ids=true, to_apply=%region_1.0 | all-reduce | flops 24 | bytes 192 | tf_op jit(solution)/shard_map/psum | solution.py:43
  19.7 0.9 fusion.5
  20.5 8.5 %all_gather.12 = bf16[24,4096]{1,0:T(8,128)(2,1)} all-gather(bf16[24,1024]{1,0:T(8,128)(2,1)S(1)} %fusion.5), channel_id=1, replica_groups=mesh['grp'=8,'voc'=4] {'voc'}, dimensions={1}, use_global_device_ids=true | all-gather | bytes 245760 | tf_op jit(solution)/shard_map/all_gather | solution.py:50
  29.1 0.7 broadcast_divide_fusion
  29.7 0.7 sign_compare_fusion
  31.2 0.9 reshape.181
  32.2 0.7 gather_fusion
  32.9 0.8 broadcast_select_fusion
  33.7 4.9 %all-to-all-start = ((bf16[8,2,2,1280]{3,2,1,0:T(2,128)(2,1)}), bf16[8,2,2,1280]{3,2,1,0:T(2,128)(2,1)S(1)}, u32[]{:S(2)}, u32[]{:S(2)}) async-start(bf16[8,2,2,1280]{3,2,1,0:T(2,128)(2,1)} %broadcast_select_fusion), calls=%async_computation | async-start | bytes 163840 | tf_op jit(solution)/shard_map/all_to_all | solution.py:26
  39.0 7.8 %all-to-all-done = bf16[8,2,2,1280]{3,2,1,0:T(2,128)(2,1)S(1)} async-done(((bf16[8,2,2,1280]{3,2,1,0:T(2,128)(2,1)}), bf16[8,2,2,1280]{3,2,1,0:T(2,128)(2,1)S(1)}, u32[]{:S(2)}, u32[]{:S(2)}) %all-to-all-start) | async-done | bytes 81952 | tf_op jit(solution)/shard_map/all_to_all | solution.py:26
  46.8 0.7 gather_fusion.1
  47.6 9.6 %all_gather.14 = bf16[24,5120]{1,0:T(8,128)(2,1)} all-gather(bf16[24,1280]{1,0:T(8,128)(2,1)S(1)} %broadcast_select_fusion.1), channel_id=1, replica_groups=mesh['grp'=8,'voc'=4] {'voc'}, dimensions={1}, use_global_device_ids=true | all-gather | bytes 307200 | tf_op jit(solution)/shard_map/all_gather | solution.py:49
  57.3 0.7 convert_divide_fusion
  58.0 0.7 fusion.11
  58.9 3.1 fusion.15
  62.0 22.9 %all-gather.5.cloned.1.call-done = bf16[192,5120]{1,0:T(8,128)(2,1)} async-done(((bf16[24,5120]{1,0:T(8,128)(2,1)}), bf16[192,5120]{1,0:T(8,128)(2,1)}) %all-gather.5.cloned.1.call-update) | async-done | bytes 1966096 | tf_op jit(solution)/shard_map/all_gather | solution.py:53
  84.9 4.0 %fusion.14 = (f32[192]{0:T(256)S(1)}, f32[192,384]{1,0:T(8,128)S(1)}) fusion(bf16[192,5120]{1,0:T(8,128)(2,1)} %all-gather.5.cloned.1.call-done, bf16[5120,384]{1,0:T(8,128)(2,1)} %param.11), kind=kOutput, calls=%fused_computation.60 | convolution fusion | flops 755048256 | bytes 6193920 | tf_op jit(solution)/shard_map/dot_general | solution.py:52
  88.9 40.2 %all-reduce.1 = (f32[192]{0:T(256)S(1)}, f32[192]{0:T(256)S(1)}) all-reduce(f32[192]{0:T(256)S(1)} %get-tuple-element.16, f32[192]{0:T(256)S(1)} %get-tuple-element.18), channel_id=1, replica_groups=mesh['grp'=8,'voc'=4] {'grp','voc'}, use_global_device_ids=true, to_apply=%region_10.11 | all-reduce | flops 384 | bytes 3072 | tf_op jit(solution)/shard_map/pmax | solution.py:65
  129.1 1.2 exponential_reduce_fusion
  130.4 39.1 %all-reduce = (f32[192]{0:T(256)S(1)}, f32[192]{0:T(256)S(1)}) all-reduce(f32[192]{0:T(256)S(1)} %get-tuple-element.20, f32[192]{0:T(256)S(1)} %get-tuple-element.21), channel_id=1, replica_groups=mesh['grp'=8,'voc'=4] {'grp','voc'}, use_global_device_ids=true, to_apply=%region_12.13 | all-reduce | flops 384 | bytes 3072 | tf_op jit(solution)/shard_map/psum | solution.py:70
  169.5 1.2 multiply_reduce_fusion
  170.7 41.0 %psum.45 = f32[192]{0:T(256)S(1)} all-reduce(f32[192]{0:T(256)S(1)} %multiply_reduce_fusion), channel_id=1, replica_groups=mesh['grp'=8,'voc'=4] {'grp','voc'}, use_global_device_ids=true, to_apply=%region_14.15 | all-reduce | flops 192 | bytes 1536 | tf_op jit(solution)/shard_map/psum | solution.py:77
  211.7 3.4 %convolution_convert_fusion.1 = bf16[192,4096]{1,0:T(8,128)(2,1)} fusion(bf16[4096,384]{1,0:T(8,128)(2,1)S(1)} %copy-done, f32[192,384]{1,0:T(8,128)} %get-tuple-element.19, f32[192,384]{1,0:T(8,128)S(1)} %get-tuple-element.17, f32[192]{0:T(256)S(1)} %psum.45, f32[192]{0:T(256)S(1)} %select_n.89, f32[192]{0:T(256)S(1)} %log_add_fusion, f32[192]{0:T(256)S(1)} %log_add_fusion.1), kind=kOutput, calls=%fused_computation.3 | convolution fusion | flops 605282304 | bytes 5311488 | tf_op jit(solution)/shard_map/dot_general | solution.py:85
  215.2 30.4 %reduce-scatter.3.cloned.1.call-done = bf16[192,1024]{1,0:T(8,128)(2,1)} async-done(((bf16[192,4096]{1,0:T(8,128)(2,1)}), bf16[192,1024]{1,0:T(8,128)(2,1)}) %reduce-scatter.3.cloned.1.call-update) | async-done | bytes 393232 | tf_op jit(solution)/shard_map/reduce_scatter | solution.py:88
  245.6 0.6 multiply_reduce_fusion.2
  246.2 4.5 %convolution_convert_fusion = bf16[4096,384]{1,0:T(8,128)(2,1)} fusion(bf16[192,4096]{1,0:T(8,128)(2,1)} %all-gather.3.cloned.1.call-done, f32[192,384]{1,0:T(8,128)} %get-tuple-element.19, f32[192,384]{1,0:T(8,128)S(1)} %get-tuple-element.17, f32[192]{0:T(256)S(1)} %psum.45, f32[192]{0:T(256)S(1)} %select_n.89, f32[192]{0:T(256)S(1)} %log_add_fusion, ...), kind=kOutput, calls=%fused_computation.2 | convolution fusion | flops 606068736 | bytes 5311488 | tf_op jit(solution)/shard_map/dot_general | solution.py:82
  250.8 27.7 %reduce-scatter.5.cloned.1.call-done = bf16[24,1024]{1,0:T(8,128)(2,1)} async-done(((bf16[192,1024]{1,0:T(8,128)(2,1)}), bf16[24,1024]{1,0:T(8,128)(2,1)}) %reduce-scatter.5.cloned.1.call-update) | async-done | bytes 49168 | tf_op jit(solution)/shard_map/reduce_scatter | solution.py:91
  278.4 1.0 fusion.10
  279.4 9.9 %psum.46 = f32[24]{0:T(128)S(1)} all-reduce(f32[24]{0:T(128)S(1)} %get-tuple-element.5), channel_id=1, replica_groups=mesh['grp'=8,'voc'=4] {'voc'}, use_global_device_ids=true, to_apply=%region_19.20 | all-reduce | flops 24 | bytes 192 | tf_op jit(solution)/shard_map/psum | solution.py:95
  289.3 14.2 %psum.47 = f32[1024]{0:T(1024)} all-reduce(f32[1024]{0:T(1024)S(1)} %get-tuple-element.4), channel_id=1, replica_groups=mesh['grp'=8,'voc'=4] {'grp'}, use_global_device_ids=true, to_apply=%region_21.22 | all-reduce | flops 1024 | bytes 8192 | tf_op jit(solution)/shard_map/psum | solution.py:99
  303.4 1.5 fusion.2
  (43 shorter events, 1.8 us)
Async XLA Ops:
  7.2 51.8 %copy-start = (bf16[4096,384]{1,0:T(8,128)(2,1)S(1)}, bf16[4096,384]{1,0:T(8,128)(2,1)}, u32[]{:S(2)}) copy-start(bf16[4096,384]{1,0:T(8,128)(2,1)} %param.10) | copy-start | bytes 9437188
  7.2 51.7 %all-gather.3.cloned.1.call-start = ((), (), s32[]{:S(2)}) async-start(), calls=%async_computation.3 | async-start | bytes 1769472 | tf_op jit(solution)/shard_map/all_gather | solution.py:58
  33.7 13.2 %all-to-all-start = ((bf16[8,2,2,1280]{3,2,1,0:T(2,128)(2,1)}), bf16[8,2,2,1280]{3,2,1,0:T(2,128)(2,1)S(1)}, u32[]{:S(2)}, u32[]{:S(2)}) async-start(bf16[8,2,2,1280]{3,2,1,0:T(2,128)(2,1)} %broadcast_select_fusion), calls=%async_computation | async-start | bytes 163840 | tf_op jit(solution)/shard_map/all_to_all | solution.py:26
  38.5 46.4 %all-gather.5.cloned.1.call-start = ((), (), s32[]{:S(2)}) async-start(), calls=%async_computation.4 | async-start | bytes 2211840 | tf_op jit(solution)/shard_map/all_gather | solution.py:53
  57.3 188.3 %reduce-scatter.3.cloned.1.call-start = ((), (), s32[]{:S(2)}) async-start(), calls=%async_computation.5 | async-start | bytes 1966080 | tf_op jit(solution)/shard_map/reduce_scatter | solution.py:88
  215.2 63.3 %reduce-scatter.5.cloned.1.call-start = ((), (), s32[]{:S(2)}) async-start(), calls=%async_computation.6 | async-start | bytes 442368 | tf_op jit(solution)/shard_map/reduce_scatter | solution.py:91
  246.2 32.2 %copy-start.1 = (bf16[24,1024]{1,0:T(8,128)(2,1)S(1)}, bf16[24,1024]{1,0:T(8,128)(2,1)}, u32[]{:S(2)}) copy-start(bf16[24,1024]{1,0:T(8,128)(2,1)} %param.7) | copy-start | bytes 147460
  246.2 32.2 %copy-start.2 = (f32[1024]{0:T(1024)S(1)}, f32[1024]{0:T(1024)}, u32[]{:S(2)}) copy-start(f32[1024]{0:T(1024)} %param.8) | copy-start | bytes 12292
Sparse Core Ops, SparseCore 0:
  29.2 27.2 all-gather.2
  58.2 26.7 all-gather.4
  215.3 30.2 reduce-scatter.2
  247.7 30.6 reduce-scatter.4
where the time goes:
time: 312 us; the launch traced here: 311 us
  blocking collectives  174 us (56%)
  waiting for transfers between devices  88.8 us (28%)
  matrix products  15.1 us (5%)
  between operations  13.9 us (4%)
  other arithmetic  11.7 us (4%)
  starting transfers between devices  5.04 us (2%)
  local copies, waits for them, and re-layouts  3.13 us (1%)
    psum x1, blocking collectives, local(): lax.psum(jnp.sum(prob_student * log_ratio, axis=1), ('grp', 'voc'))  41 us
    pmax x1, blocking collectives, local(): lax.pmax((jnp.max(student_logits, axis=1), jnp.max(teacher_logits, axis=1...  40.2 us
    psum x1, blocking collectives, local(): lax.psum((jnp.sum(exp_student, axis=1), jnp.sum(exp_teacher, axis=1)), ('...  39.1 us
    reduce_scatter x1, waiting for transfers between devices, local(): lax.psum_scatter(full_term.astype(jnp.bfloat16), 'voc', scatter_dimension...  30.4 us
    reduce_scatter x1, waiting for transfers between devices, local(): lax.psum_scatter(feature_part, 'grp', scatter_dimension=0, tiled=True)  27.7 us
    all_gather x1, waiting for transfers between devices, local(): lax.all_gather(teacher_rows, 'grp', axis=0, tiled=True)  22.9 us
    psum x1, blocking collectives, local(): lax.psum(jnp.sum(normed_grad * hidden_f32 * inverse_rms[:, None], axis=0)...  14.2 us
    psum x1, blocking collectives, local(): squares = lax.psum(jnp.sum(hidden_f32 * hidden_f32, axis=1), 'voc')  11.4 us
  transfers between devices with their start and end apart: 5, of which 4 were waited for; matrix products, arithmetic and copies ran while one was open for 5% of the time, Pallas kernels for 0%

commit v1 on v0

--- a/solution.py
+++ b/solution.py
@@ -1,6 +1,10 @@
+import functools
+
 import jax
 import jax.numpy as jnp
 from jax import lax
+from jax.experimental import pallas as pl
+from jax.experimental.pallas import tpu as pltpu
 from jax.sharding import PartitionSpec as P
 
 DS = 4096
@@ -9,6 +13,361 @@
 
 
 EPSILON = 1e-06
+
+F32 = jnp.float32
+BF16 = jnp.bfloat16
+MESH = pl.DeviceIdType.MESH
+
+
+def flip(number, mask):
+    low, high = number % 2, number // 2
+    if mask & 1:
+        low = 1 - low
+    if mask & 2:
+        high = 1 - high
+    return high * 2 + low
+
+
+def merge(parts):
+    top = functools.reduce(jnp.maximum, [p[0:1] for p in parts])
+    top_t = functools.reduce(jnp.maximum, [p[2:3] for p in parts])
+    total = total_t = ratio = logit = both = 0.0
+    for p in parts:
+        shift, shift_t = p[0:1] - top, p[2:3] - top_t
+        factor, factor_t = jnp.exp(shift), jnp.exp(shift_t)
+        live = factor > 0.0
+        shift = jnp.where(live, shift, 0.0)
+        gap = shift - jnp.where(live, shift_t, 0.0)
+        total = total + factor * p[1:2]
+        total_t = total_t + factor_t * p[3:4]
+        ratio = ratio + factor * (p[4:5] + p[1:2] * gap)
+        logit = logit + factor * (p[5:6] + p[1:2] * shift)
+        both = both + factor * (p[6:7] + gap * p[5:6] + shift * p[4:5] + shift * gap * p[1:2])
+    return jnp.concatenate([top, total, top_t, total_t, ratio, logit, both, jnp.zeros_like(top)], axis=0)
+
+
+def kernel(
+    sh_ref, th_ref, gain_ref, order_ref, weight_ref, w_hbm, t_hbm,
+    loss_ref, gh_ref, gg_ref, head_hbm,
+    wv, tv, sx, tx, in_s, in_t, s_blk, t_blk, hg, s_acc, t_acc, sq, cols,
+    st_a, st_b, g2, own, p_sib, r_sib, p_x, r_x, rb, rz, gp, gz, head,
+    w_sem, t_sem, h_sem, s1s, s1r, t1s, t1r, s2s, s2r, t2s, t2r, as_, ar, bs, br,
+    qs, qr, xs, xr, zs, zr, ys, yr,
+):
+    g = lax.axis_index("grp")
+    v = lax.axis_index("voc")
+    z, c = g // 2, g % 2
+    k = v * 2 + c
+    rows, half_s = in_s.shape[1], in_s.shape[2]
+    half_t = in_t.shape[2]
+    tokens = s_acc.shape[0]
+
+    def plane(vm, cm):
+        return {"grp": z * 2 + (1 - c if cm else c), "voc": flip(v, vm)}
+
+    def column(zm, cm):
+        return {"grp": flip(z, zm) * 2 + (1 - c if cm else c), "voc": v}
+
+    def slot(vm, cm):
+        return flip(v, vm) * 2 + (1 - c if cm else c)
+
+    sends = []
+
+    def send(src, dst, ssem, rsem, to):
+        copy = pltpu.make_async_remote_copy(
+            src_ref=src, dst_ref=dst, send_sem=ssem, recv_sem=rsem, device_id=to, device_id_type=MESH
+        )
+        copy.start()
+        sends.append(copy)
+
+    def arrived(dst, ssem, rsem, to):
+        pltpu.make_async_remote_copy(
+            src_ref=dst, dst_ref=dst, send_sem=ssem, recv_sem=rsem, device_id=to, device_id_type=MESH
+        ).wait_recv()
+
+    w_copy = pltpu.make_async_copy(w_hbm, wv, w_sem)
+    t_copy = pltpu.make_async_copy(t_hbm, tv, t_sem)
+    w_copy.start()
+    t_copy.start()
+
+    barrier = pltpu.get_barrier_semaphore()
+    peers = [plane(m // 2, m % 2) for m in range(1, 8)] + [column(m // 2, m % 2) for m in range(2, 8)]
+    for peer in peers:
+        pl.semaphore_signal(barrier, inc=1, device_id=peer, device_id_type=MESH)
+    for h in range(2):
+        sx[h] = sh_ref[:, h * half_s:(h + 1) * half_s]
+        tx[h] = th_ref[:, h * half_t:(h + 1) * half_t]
+    pl.semaphore_wait(barrier, len(peers))
+
+    for m in range(1, 8):
+        other = 1 - c if m % 2 else c
+        send(sx.at[other], in_s.at[g], s1s.at[m], s1r.at[m], column(m // 2, m % 2))
+    for m in range(1, 8):
+        other = 1 - c if m % 2 else c
+        send(tx.at[other], in_t.at[g], t1s.at[m], t1r.at[m], column(m // 2, m % 2))
+    in_s[g] = sx[c]
+    in_t[g] = tx[c]
+    gain = gain_ref[...]
+    own_gain = jnp.where(c == 0, gain[:, :half_s], gain[:, half_s:])
+    hi = own_gain.astype(BF16).astype(F32)
+    mid = (own_gain - hi).astype(BF16).astype(F32)
+    lo = own_gain - hi - mid
+    line = lax.broadcasted_iota(jnp.int32, (16, half_s), 0)
+    gain_rows = jnp.where(line == 0, hi, jnp.where(line == 1, mid, jnp.where(line == 2, lo, 0.0)))
+    s_blk[k, tokens:, :] = gain_rows.astype(BF16)
+
+    def source(m):
+        return flip(z, m // 2) * 2 + (1 - c if m % 2 else c)
+
+    for m in range(1, 8):
+        arrived(in_s.at[source(m)], s1s.at[m], s1r.at[m], column(m // 2, m % 2))
+    s_blk[k, :tokens, :] = jnp.concatenate([in_s[i].astype(F32) for i in range(8)], axis=0).astype(BF16)
+    for vm in (1, 2, 3):
+        send(s_blk.at[k], s_blk.at[k], s2s.at[vm * 2], s2r.at[vm * 2], plane(vm, 0))
+    send(s_blk.at[k], s_blk.at[k], s2s.at[1], s2r.at[1], plane(0, 1))
+    for m in range(1, 8):
+        arrived(in_t.at[source(m)], t1s.at[m], t1r.at[m], column(m // 2, m % 2))
+    t_blk[k] = jnp.concatenate([in_t[i].astype(F32) for i in range(8)], axis=0).astype(BF16)
+    for vm in (1, 2, 3):
+        send(t_blk.at[k], t_blk.at[k], t2s.at[vm * 2], t2r.at[vm * 2], plane(vm, 0))
+    send(t_blk.at[k], t_blk.at[k], t2s.at[1], t2r.at[1], plane(0, 1))
+
+    s_acc[...] = jnp.zeros_like(s_acc)
+    t_acc[...] = jnp.zeros_like(t_acc)
+    sq[...] = jnp.zeros_like(sq)
+    w_copy.wait()
+
+    def student_block(at):
+        x = s_blk[at, :tokens, :].astype(F32)
+        tail = s_blk[at, tokens:, :].astype(F32)
+        scale = jnp.sum(tail, axis=0, keepdims=True)
+        squares = x * x
+        partial = squares[:, 0:128]
+        for i in range(1, half_s // 128):
+            partial = partial + squares[:, i * 128:(i + 1) * 128]
+        sq[...] += partial
+        scaled = (x * scale).astype(BF16)
+        hg[at] = scaled
+        s_acc[...] += jnp.dot(scaled, wv[at], preferred_element_type=F32)
+
+    def teacher_block(at):
+        t_acc[...] += jnp.dot(t_blk[at], tv[at], preferred_element_type=F32)
+
+    def relay(blk, ssem, rsem, vm):
+        at = slot(vm, 0)
+        arrived(blk.at[at], ssem.at[vm * 2], rsem.at[vm * 2], plane(vm, 0))
+        send(blk.at[at], blk.at[at], ssem.at[vm * 2 + 1], rsem.at[vm * 2 + 1], plane(0, 1))
+
+    def sibling(blk, ssem, rsem, vm):
+        arrived(blk.at[slot(vm, 1)], ssem.at[vm * 2 + 1], rsem.at[vm * 2 + 1], plane(0, 1))
+
+    student_block(k)
+    t_copy.wait()
+    teacher_block(k)
+    sibling(s_blk, s2s, s2r, 0)
+    student_block(slot(0, 1))
+    sibling(t_blk, t2s, t2r, 0)
+    teacher_block(slot(0, 1))
+    for vm in (1, 2, 3):
+        relay(s_blk, s2s, s2r, vm)
+        student_block(slot(vm, 0))
+        sibling(s_blk, s2s, s2r, vm)
+        student_block(slot(vm, 1))
+    for vm in (1, 2, 3):
+        relay(t_blk, t2s, t2r, vm)
+        teacher_block(slot(vm, 0))
+        sibling(t_blk, t2s, t2r, vm)
+        teacher_block(slot(vm, 1))
+
+    inv = lax.rsqrt(jnp.sum(sq[...], axis=1, keepdims=True) / DS + EPSILON)
+    s_log = s_acc[...] * inv
+    raw = t_acc[...]
+    pick = (order_ref[...] == lax.broadcasted_iota(jnp.int32, (tokens, tokens), 1)).astype(F32).astype(BF16)
+    part0 = raw.astype(BF16)
+    rest = raw - part0.astype(F32)
+    part1 = rest.astype(BF16)
+    part2 = (rest - part1.astype(F32)).astype(BF16)
+    t_log = (
+        jnp.dot(pick, part0, preferred_element_type=F32)
+        + jnp.dot(pick, part1, preferred_element_type=F32)
+        + jnp.dot(pick, part2, preferred_element_type=F32)
+    )
+    top = jnp.max(s_log, axis=1, keepdims=True)
+    top_t = jnp.max(t_log, axis=1, keepdims=True)
+    a = s_log - top
+    b = t_log - top_t
+    e = jnp.exp(a)
+    ea = e * a
+    d = a - b
+    figures = [
+        top, jnp.sum(e, axis=1, keepdims=True), top_t, jnp.sum(jnp.exp(b), axis=1, keepdims=True),
+        jnp.sum(e * d, axis=1, keepdims=True), jnp.sum(ea, axis=1, keepdims=True),
+        jnp.sum(ea * d, axis=1, keepdims=True),
+    ]
+    lane = lax.broadcasted_iota(jnp.int32, (tokens, 128), 1)
+    packed = jnp.zeros((tokens, 128), F32)
+    for i, figure in enumerate(figures):
+        packed = jnp.where(lane == i, figure, packed)
+    packed = jnp.concatenate([packed, jnp.zeros((256 - tokens, 128), F32)], axis=0)
+    st_a[k] = jnp.transpose(packed)[0:8, :]
+    for m in range(1, 8):
+        send(st_a.at[k], st_a.at[k], as_.at[m], ar.at[m], plane(m // 2, m % 2))
+    for m in range(1, 8):
+        arrived(st_a.at[slot(m // 2, m % 2)], as_.at[m], ar.at[m], plane(m // 2, m % 2))
+    st_b[z] = merge([st_a[i] for i in range(8)])
+    for m in range(1, 4):
+        send(st_b.at[z], st_b.at[z], bs.at[m], br.at[m], column(m, 0))
+    for m in range(1, 4):
+        arrived(st_b.at[flip(z, m)], bs.at[m], br.at[m], column(m, 0))
+    full = merge([st_b[i] for i in range(4)])
+    total = full[1:2]
+    lse = full[0:1] + jnp.log(total)
+    lse_t = full[2:3] + jnp.log(full[3:4])
+    mean_ratio, mean_logit = full[4:5] / total, full[5:6] / total
+    divergence = mean_ratio - jnp.log(total) + jnp.log(full[3:4])
+    offset = lse - lse_t + divergence
+    cov = full[6:7] / total - mean_ratio * mean_logit
+    back = jnp.concatenate([lse, offset, divergence, cov, jnp.zeros((124, 256), F32)], axis=0)
+    back = jnp.transpose(back)[:tokens]
+    weight = weight_ref[...]
+    loss_ref[...] = jnp.sum(weight * back[:, 2:3], axis=0, keepdims=True)
+    prob = jnp.exp(s_log - back[:, 0:1])
+    grad = ((weight * inv) * prob * (s_log - t_log - back[:, 1:2])).astype(BF16)
+    g2[...] = grad
+    lane = lax.broadcasted_iota(jnp.int32, (tokens, 128), 1)
+    cols[...] = jnp.where(lane == 0, weight * inv * inv * back[:, 3:4] / DS, 0.0)
+
+    def block_grad(at):
+        return lax.dot_general(g2[...], wv[at], (((1,), (1,)), ((), ())), preferred_element_type=F32)
+
+    order = (1, 2, 3, 0)
+    for vm in order:
+        p_sib[vm] = block_grad(slot(vm, 1)).astype(BF16)
+        send(p_sib.at[vm], r_sib.at[vm], qs.at[vm], qr.at[vm], plane(0, 1))
+    for vm in order:
+        mine = block_grad(slot(vm, 0))
+        arrived(r_sib.at[vm], qs.at[vm], qr.at[vm], plane(0, 1))
+        mine = mine + r_sib[vm].astype(F32)
+        if vm:
+            p_x[vm] = mine.astype(BF16)
+            send(p_x.at[vm], r_x.at[vm], xs.at[vm], xr.at[vm], plane(vm, 0))
+        else:
+            own[...] = mine
+
+    head_copies = []
+    for i in range(8):
+        head[i] = lax.dot_general(
+            hg[i], g2[...], (((0,), (0,)), ((), ())), preferred_element_type=F32
+        ).astype(BF16)
+        copy = pltpu.make_async_copy(head.at[i], head_hbm.at[i], h_sem.at[i])
+        copy.start()
+        head_copies.append(copy)
+
+    for vm in (1, 2, 3):
+        arrived(r_x.at[vm], xs.at[vm], xr.at[vm], plane(vm, 0))
+    total = own[...]
+    for vm in (1, 2, 3):
+        total = total + r_x[vm].astype(F32)
+    for i in range(8):
+        rb[i] = total[i * rows:(i + 1) * rows].astype(BF16)
+    for m in range(1, 8):
+        send(rb.at[source(m)], rz.at[g], zs.at[m], zr.at[m], column(m // 2, m % 2))
+    rz[g] = rb[g]
+    prod = total * s_blk[k, :tokens, :].astype(F32)
+    part = prod[0:8]
+    for i in range(1, tokens // 8):
+        part = part + prod[i * 8:(i + 1) * 8]
+    gp[...] = part
+    for m in range(1, 8):
+        send(gp, gz.at[g], ys.at[m], yr.at[m], column(m // 2, m % 2))
+    gz[g] = part
+    for m in range(1, 8):
+        arrived(rz.at[source(m)], zs.at[m], zr.at[m], column(m // 2, m % 2))
+    own_cols = cols[pl.ds(pl.multiple_of(g * rows, 8), rows), :][:, 0:1]
+    for h in range(2):
+        at = slice(h * half_s, (h + 1) * half_s)
+        ng = rz[h].astype(F32)
+        for i in range(1, 4):
+            ng = ng + rz[2 * i + h].astype(F32)
+        hid = sh_ref[:, at].astype(F32)
+        gh_ref[:, at] = (gain_ref[:, at] * ng - hid * own_cols).astype(BF16)
+    for m in range(1, 8):
+        arrived(gz.at[source(m)], ys.at[m], yr.at[m], column(m // 2, m % 2))
+    for h in range(2):
+        at = slice(h * half_s, (h + 1) * half_s)
+        ng = gz[h]
+        for i in range(1, 4):
+            ng = ng + gz[2 * i + h]
+        gg_ref[:, at] = jnp.sum(ng, axis=0, keepdims=True)
+    for copy in head_copies:
+        copy.wait()
+    for copy in sends:
+        copy.wait_send()
+
+
+def fused(
+    student_hidden, norm_gain, teacher_hidden, student_head, teacher_head, episode_source, lengths
+):
+    rows, wide_s = student_hidden.shape
+    wide_t = teacher_hidden.shape[1]
+    tokens = rows * lax.axis_size("grp")
+    voc = student_head.shape[1]
+    half_s, half_t = wide_s // 2, wide_t // 2
+    positions = jnp.arange(SEQ, dtype=jnp.int32)
+    order = (episode_source[:, None] * SEQ + positions[None, :]).reshape(-1, 1)
+    valid = positions[None, :] < lengths[:, None]
+    weight = jnp.where(valid, 1.0 / lengths.astype(F32)[:, None], 0.0).reshape(-1, 1)
+    vmem = pl.BlockSpec(memory_space=pltpu.VMEM)
+    hbm = pl.BlockSpec(memory_space=pl.ANY)
+    dma = pltpu.SemaphoreType.DMA
+    loss, grad_hidden, grad_gain, grad_head = pl.pallas_call(
+        kernel,
+        out_shape=(
+            jax.ShapeDtypeStruct((1, 1), F32),
+            jax.ShapeDtypeStruct((rows, wide_s), BF16),
+            jax.ShapeDtypeStruct((1, wide_s), F32),
+            jax.ShapeDtypeStruct((8, half_s, voc), BF16),
+        ),
+        in_specs=[vmem] * 5 + [hbm] * 2,
+        out_specs=(vmem, vmem, vmem, hbm),
+        scratch_shapes=[
+            pltpu.VMEM((8, half_s, voc), BF16),
+            pltpu.VMEM((8, half_t, voc), BF16),
+            pltpu.VMEM((2, rows, half_s), BF16),
+            pltpu.VMEM((2, rows, half_t), BF16),
+            pltpu.VMEM((8, rows, half_s), BF16),
+            pltpu.VMEM((8, rows, half_t), BF16),
+            pltpu.VMEM((8, tokens + 16, half_s), BF16),
+            pltpu.VMEM((8, tokens, half_t), BF16),
+            pltpu.VMEM((8, tokens, half_s), BF16),
+            pltpu.VMEM((tokens, voc), F32),
+            pltpu.VMEM((tokens, voc), F32),
+            pltpu.VMEM((tokens, 128), F32),
+            pltpu.VMEM((tokens, 128), F32),
+            pltpu.VMEM((8, 8, 256), F32),
+            pltpu.VMEM((4, 8, 256), F32),
+            pltpu.VMEM((tokens, voc), BF16),
+            pltpu.VMEM((tokens, half_s), F32),
+            pltpu.VMEM((4, tokens, half_s), BF16),
+            pltpu.VMEM((4, tokens, half_s), BF16),
+            pltpu.VMEM((4, tokens, half_s), BF16),
+            pltpu.VMEM((4, tokens, half_s), BF16),
+            pltpu.VMEM((8, rows, half_s), BF16),
+            pltpu.VMEM((8, rows, half_s), BF16),
+            pltpu.VMEM((8, half_s), F32),
+            pltpu.VMEM((8, 8, half_s), F32),
+            pltpu.VMEM((8, half_s, voc), BF16),
+            dma(()), dma(()), dma((8,)),
+        ] + [dma((8,))] * 20,
+        compiler_params=pltpu.CompilerParams(
+            collective_id=0, has_side_effects=True, vmem_limit_bytes=52 * 1024 * 1024
+        ),
+        cost_estimate=pl.CostEstimate(flops=2600000000, bytes_accessed=11000000, transcendentals=400000),
+    )(
+        student_hidden, teacher_hidden, norm_gain.reshape(1, -1), order, weight,
+        student_head.reshape(8, half_s, voc), teacher_head.reshape(8, half_t, voc),
+    )
+    return (loss[0, 0], grad_hidden, grad_gain.reshape(-1), grad_head.reshape(student_head.shape))
 
 
 def realign(teacher_hidden, table, group_index, per_group):
@@ -110,8 +469,9 @@
         P(),
         P(),
     )
+    body = fused if tuple(mesh.shape.values()) == (8, 4) else local
     return jax.shard_map(
-        local,
+        body,
         mesh=mesh,
         in_specs=placed,
         out_specs=(P(), P("grp", "voc"), P("voc"), P(None, ("grp", "voc"))),

time: 312 us -> 79.5 us (0.25)
  blocking collectives: 174 us -> 0 us
  waiting for transfers between devices: 88.8 us -> 0 us
  Pallas kernels: 0 us -> 67.1 us
  matrix products: 15.1 us -> 0 us
  between operations: 13.9 us -> 2.33 us
  other arithmetic: 11.7 us -> 2.13 us
  starting transfers between devices: 5.04 us -> 0 us
  local copies, waits for them, and re-layouts: 3.13 us -> 7.57 us
    psum x5 -> x0, blocking collectives: 115 us -> none  [the longest x1 41 us: local(): lax.psum(jnp.sum(prob_student * log_ratio, axis=1), ('grp', 'voc'))]
    pallas_call x0 -> x1, Pallas kernels: none -> 67.1 us  [fused(): pl.pallas_call(kernel, out_shape=(jax.ShapeDtypeStruct((1, 1), F32), jax....]
    reduce_scatter x2 -> x0, waiting for transfers between devices: 58 us -> none  [the longest x1 30.4 us: local(): lax.psum_scatter(full_term.astype(jnp.bfloat16), 'voc', scatter_dimension...]
    pmax x1 -> x0, blocking collectives: 40.2 us -> none  [local(): lax.pmax((jnp.max(student_logits, axis=1), jnp.max(teacher_logits, axis=1...]
    all_gather x2 -> x0, waiting for transfers between devices: 22.9 us -> none  [the longest x1 22.9 us: local(): lax.all_gather(teacher_rows, 'grp', axis=0, tiled=True)]
    all_gather x2 -> x0, blocking collectives: 18.1 us -> none  [the longest x1 9.63 us: local(): lax.all_gather(aligned, 'voc', axis=1, tiled=True)]
    dot_general x4 -> x0, matrix products: 15.1 us -> none  [the longest x1 4.55 us: local(): lax.dot_general(all_rows, logit_grad, (((0,), (0,)), ((), ())), preferred...]
    all_to_all x1 -> x0, waiting for transfers between devices: 7.82 us -> none  [realign(): lax.all_to_all(outgoing, 'grp', split_axis=0, concat_axis=0, tiled=True)]
  transfers between devices with their start and end apart: 5 -> 0, of which waited for: 4 -> 0; matrix products, arithmetic and copies ran while one was open for 5% -> 0% of each run, Pallas kernels for 0% -> 0%
where the time goes in v1:
time: 79.5 us; the launch traced here: 79.1 us
  Pallas kernels  67.1 us (84%)
  local copies, waits for them, and re-layouts  7.57 us (10%)
  between operations  2.33 us (3%)
  other arithmetic  2.13 us (3%)
    pallas_call x1, Pallas kernels, fused(): pl.pallas_call(kernel, out_shape=(jax.ShapeDtypeStruct((1, 1), F32), jax....  67.1 us
    unnamed x9, local copies, waits for them, and re-layouts  7.41 us

profile of v1, /device:TPU:0, one launch (start us, length us, event | category | flops | bytes accessed | tf_op | source)
XLA Modules:
  0.0 79.1 jit_solution(12136145428704412010)
XLA Ops:
  0.6 0.7 broadcast_multiply_fusion
  1.3 0.7 convert_divide_fusion
  1.9 0.7 fusion
  2.7 0.1 iota_add_fusion
  2.8 0.1 add.30.order_ref
  2.9 0.1 select_n.16.weight_ref
  2.9 0.0 copy-start
  2.9 0.8 %copy-done = bf16[24,1280]{1,0:T(8,128)(2,1)S(1)} copy-done((bf16[24,1280]{1,0:T(8,128)(2,1)S(1)}, bf16[24,1280]{1,0:T(8,128)(2,1)}, u32[]{:S(2)}) %copy-start) | copy-done | bytes 61464
  3.8 0.0 copy-start.1
  3.8 0.8 %copy-done.1 = bf16[24,1024]{1,0:T(8,128)(2,1)S(1)} copy-done((bf16[24,1024]{1,0:T(8,128)(2,1)S(1)}, bf16[24,1024]{1,0:T(8,128)(2,1)}, u32[]{:S(2)}) %copy-start.1) | copy-done | bytes 49176
  4.6 0.0 copy-start.2
  4.6 0.7 copy-done.2
  5.3 67.1 %shard_map.102 = (f32[1,1]{1,0:T(1,128)}, bf16[24,1024]{1,0:T(8,128)(2,1)S(1)}, f32[1,1024]{1,0:T(1,128)S(1)}, bf16[8,512,384]{2,1,0:T(8,128)(2,1)}) custom-call(bf16[24,1024]{1,0:T(8,128)(2,1)S(1)} %copy-done.1, bf16[24,1280]{1,0:T(8,128)(2,1)S(1)} %copy-done, f32[1,1024]{1,0:T(1,128)S(1)} %bitcast.7, s32[192,1]{1,0:T(8,128)S(1)} %add.30.order_ref, ...), custom_call_target="tpu_custom_call" | custom-call | flops 2600000000 | bytes 11000000 | tf_op jit(solution)/shard_map/pallas_call | solution.py:323
  72.9 0.6 copy.18
  73.5 0.6 copy.19
  74.1 3.9 %copy.20 = bf16[4096,384]{1,0:T(8,128)(2,1)} copy(bf16[4096,384]{1,0:T(8,128)(2,1)} %bitcast.8) | data formatting | bytes 6291456
Async XLA Ops:
  2.9 0.8 %copy-start = (bf16[24,1280]{1,0:T(8,128)(2,1)S(1)}, bf16[24,1280]{1,0:T(8,128)(2,1)}, u32[]{:S(2)}) copy-start(bf16[24,1280]{1,0:T(8,128)(2,1)} %th_ref.1) | copy-start | bytes 184324
  3.8 0.8 %copy-start.1 = (bf16[24,1024]{1,0:T(8,128)(2,1)S(1)}, bf16[24,1024]{1,0:T(8,128)(2,1)}, u32[]{:S(2)}) copy-start(bf16[24,1024]{1,0:T(8,128)(2,1)} %sh_ref.1) | copy-start | bytes 147460
  4.6 0.7 copy-start.2

commit v2 on v1

--- a/solution.py
+++ b/solution.py
@@ -16,6 +16,7 @@
 
 F32 = jnp.float32
 BF16 = jnp.bfloat16
+LIMIT = 65472
 MESH = pl.DeviceIdType.MESH
 
 
@@ -47,11 +48,11 @@
 
 
 def kernel(
-    sh_ref, th_ref, gain_ref, order_ref, weight_ref, w_hbm, t_hbm,
-    loss_ref, gh_ref, gg_ref, head_hbm,
-    wv, tv, sx, tx, in_s, in_t, s_blk, t_blk, hg, s_acc, t_acc, sq, cols,
-    st_a, st_b, g2, own, p_sib, r_sib, p_x, r_x, rb, rz, gp, gz, head,
-    w_sem, t_sem, h_sem, s1s, s1r, t1s, t1r, s2s, s2r, t2s, t2r, as_, ar, bs, br,
+    sh_hbm, th_hbm, gain_hbm, source_hbm, lengths_hbm, w_hbm, t_hbm,
+    loss_ref, gh_ref, gg_ref, hg, g2,
+    wv, tv, sh_ref, gain_ref, source_ref, lengths_ref, pick_ref, in_s, in_t, s_blk, t_blk, s_acc, t_acc, sq, cols,
+    st_a, st_b, own, p_sib, r_sib, p_x, r_x, rb, rz, gp, gz,
+    w_sem, t_sem, l_sem, s1s, s1r, t1s, t1r, s2s, s2r, t2s, t2r, as_, ar, bs, br,
     qs, qr, xs, xr, zs, zr, ys, yr,
 ):
     g = lax.axis_index("grp")
@@ -60,7 +61,9 @@
     k = v * 2 + c
     rows, half_s = in_s.shape[1], in_s.shape[2]
     half_t = in_t.shape[2]
-    tokens = s_acc.shape[0]
+    tokens = in_s.shape[0] * rows
+    valid = tokens * 5 // 8
+    slots = s_acc.shape[0]
 
     def plane(vm, cm):
         return {"grp": z * 2 + (1 - c if cm else c), "voc": flip(v, vm)}
@@ -85,6 +88,18 @@
             src_ref=dst, dst_ref=dst, send_sem=ssem, recv_sem=rsem, device_id=to, device_id_type=MESH
         ).wait_recv()
 
+    def half(ref, number, width):
+        return ref.at[:, pl.ds(pl.multiple_of(number * width, 128), width)]
+
+    local_copies = [
+        pltpu.make_async_copy(src, dst, l_sem.at[i])
+        for i, (src, dst) in enumerate((
+            (source_hbm, source_ref), (lengths_hbm, lengths_ref), (gain_hbm, gain_ref),
+            (half(sh_hbm, c, half_s), in_s.at[g]), (half(th_hbm, c, half_t), in_t.at[g]), (sh_hbm, sh_ref),
+        ))
+    ]
+    for copy in local_copies:
+        copy.start()
     w_copy = pltpu.make_async_copy(w_hbm, wv, w_sem)
     t_copy = pltpu.make_async_copy(t_hbm, tv, t_sem)
     w_copy.start()
@@ -94,40 +109,71 @@
     peers = [plane(m // 2, m % 2) for m in range(1, 8)] + [column(m // 2, m % 2) for m in range(2, 8)]
     for peer in peers:
         pl.semaphore_signal(barrier, inc=1, device_id=peer, device_id_type=MESH)
-    for h in range(2):
-        sx[h] = sh_ref[:, h * half_s:(h + 1) * half_s]
-        tx[h] = th_ref[:, h * half_t:(h + 1) * half_t]
     pl.semaphore_wait(barrier, len(peers))
 
     for m in range(1, 8):
         other = 1 - c if m % 2 else c
-        send(sx.at[other], in_s.at[g], s1s.at[m], s1r.at[m], column(m // 2, m % 2))
+        send(half(sh_hbm, other, half_s), in_s.at[g], s1s.at[m], s1r.at[m], column(m // 2, m % 2))
     for m in range(1, 8):
         other = 1 - c if m % 2 else c
-        send(tx.at[other], in_t.at[g], t1s.at[m], t1r.at[m], column(m // 2, m % 2))
-    in_s[g] = sx[c]
-    in_t[g] = tx[c]
+        send(half(th_hbm, other, half_t), in_t.at[g], t1s.at[m], t1r.at[m], column(m // 2, m % 2))
+
+    for copy in local_copies[:3]:
+        copy.wait()
+    episodes = source_ref.shape[1]
+    line = lax.broadcasted_iota(jnp.int32, (8, episodes), 0)
+    table = jnp.where(line == 0, source_ref[...], jnp.where(line == 1, lengths_ref[...], 0)).astype(F32).astype(BF16)
+    spread = lax.broadcasted_iota(jnp.int32, (episodes, tokens), 1) // SEQ == lax.broadcasted_iota(
+        jnp.int32, (episodes, tokens), 0
+    )
+    table = jnp.dot(table, spread.astype(F32).astype(BF16), preferred_element_type=F32)
+    position = (lax.broadcasted_iota(jnp.int32, (1, tokens), 1) % SEQ).astype(F32)
+    row_source = table[0:1] * SEQ + position
+    row_length = table[1:2]
+    row_valid = (position < row_length).astype(F32)
+    before = lax.broadcasted_iota(jnp.int32, (tokens, tokens), 0) < lax.broadcasted_iota(jnp.int32, (tokens, tokens), 1)
+    rank = jnp.dot(
+        jnp.broadcast_to(row_valid, (8, tokens)).astype(BF16), before.astype(F32).astype(BF16),
+        preferred_element_type=F32,
+    )[0:1]
+    slot_line = lax.broadcasted_iota(jnp.int32, (slots, tokens), 0).astype(F32)
+    pick = jnp.where(slot_line == rank, row_valid, 0.0).astype(BF16)
+    pick_ref[...] = pick
+    line = lax.broadcasted_iota(jnp.int32, (8, tokens), 0)
+    both = jnp.where(line == 0, row_source, jnp.where(line == 1, row_length, 0.0)).astype(BF16)
+    slot_table = lax.dot_general(pick, both, (((1,), (1,)), ((), ())), preferred_element_type=F32)
+    slot_source, slot_length = slot_table[:, 0:1], slot_table[:, 1:2]
+    weight = jnp.where(slot_length > 0.0, 1.0 / jnp.maximum(slot_length, 1.0), 0.0)
+    teacher_lane = lax.broadcasted_iota(jnp.int32, (slots, tokens), 1).astype(F32)
+    pick_t = jnp.where((slot_source == teacher_lane) & (slot_length > 0.0), 1.0, 0.0).astype(BF16)
+
     gain = gain_ref[...]
     own_gain = jnp.where(c == 0, gain[:, :half_s], gain[:, half_s:])
     hi = own_gain.astype(BF16).astype(F32)
     mid = (own_gain - hi).astype(BF16).astype(F32)
     lo = own_gain - hi - mid
-    line = lax.broadcasted_iota(jnp.int32, (16, half_s), 0)
-    gain_rows = jnp.where(line == 0, hi, jnp.where(line == 1, mid, jnp.where(line == 2, lo, 0.0)))
-    s_blk[k, tokens:, :] = gain_rows.astype(BF16)
+    slot_id = lax.broadcasted_iota(jnp.int32, (slots, half_s), 0)
+    gain_rows = jnp.where(
+        slot_id == valid, hi, jnp.where(slot_id == valid + 1, mid, jnp.where(slot_id == valid + 2, lo, 0.0))
+    )
 
     def source(m):
         return flip(z, m // 2) * 2 + (1 - c if m % 2 else c)
 
     for m in range(1, 8):
         arrived(in_s.at[source(m)], s1s.at[m], s1r.at[m], column(m // 2, m % 2))
-    s_blk[k, :tokens, :] = jnp.concatenate([in_s[i].astype(F32) for i in range(8)], axis=0).astype(BF16)
+    for copy in local_copies[3:]:
+        copy.wait()
+    block = jnp.concatenate([in_s[i].astype(F32) for i in range(8)], axis=0).astype(BF16)
+    block = jnp.dot(pick, block, preferred_element_type=F32)
+    s_blk[k] = jnp.where(slot_id < valid, block, gain_rows).astype(BF16)
     for vm in (1, 2, 3):
         send(s_blk.at[k], s_blk.at[k], s2s.at[vm * 2], s2r.at[vm * 2], plane(vm, 0))
     send(s_blk.at[k], s_blk.at[k], s2s.at[1], s2r.at[1], plane(0, 1))
     for m in range(1, 8):
         arrived(in_t.at[source(m)], t1s.at[m], t1r.at[m], column(m // 2, m % 2))
-    t_blk[k] = jnp.concatenate([in_t[i].astype(F32) for i in range(8)], axis=0).astype(BF16)
+    block = jnp.concatenate([in_t[i].astype(F32) for i in range(8)], axis=0).astype(BF16)
+    t_blk[k] = jnp.dot(pick_t, block, preferred_element_type=F32).astype(BF16)
     for vm in (1, 2, 3):
         send(t_blk.at[k], t_blk.at[k], t2s.at[vm * 2], t2r.at[vm * 2], plane(vm, 0))
     send(t_blk.at[k], t_blk.at[k], t2s.at[1], t2r.at[1], plane(0, 1))
@@ -138,9 +184,9 @@
     w_copy.wait()
 
     def student_block(at):
-        x = s_blk[at, :tokens, :].astype(F32)
-        tail = s_blk[at, tokens:, :].astype(F32)
-        scale = jnp.sum(tail, axis=0, keepdims=True)
+        x = s_blk[at].astype(F32)
+        scale = jnp.sum(x[valid:], axis=0, keepdims=True)
+        x = jnp.where(slot_id < valid, x, 0.0)
         squares = x * x
         partial = squares[:, 0:128]
         for i in range(1, half_s // 128):
@@ -181,17 +227,7 @@
 
     inv = lax.rsqrt(jnp.sum(sq[...], axis=1, keepdims=True) / DS + EPSILON)
     s_log = s_acc[...] * inv
-    raw = t_acc[...]
-    pick = (order_ref[...] == lax.broadcasted_iota(jnp.int32, (tokens, tokens), 1)).astype(F32).astype(BF16)
-    part0 = raw.astype(BF16)
-    rest = raw - part0.astype(F32)
-    part1 = rest.astype(BF16)
-    part2 = (rest - part1.astype(F32)).astype(BF16)
-    t_log = (
-        jnp.dot(pick, part0, preferred_element_type=F32)
-        + jnp.dot(pick, part1, preferred_element_type=F32)
-        + jnp.dot(pick, part2, preferred_element_type=F32)
-    )
+    t_log = t_acc[...]
     top = jnp.max(s_log, axis=1, keepdims=True)
     top_t = jnp.max(t_log, axis=1, keepdims=True)
     a = s_log - top
@@ -204,11 +240,10 @@
         jnp.sum(e * d, axis=1, keepdims=True), jnp.sum(ea, axis=1, keepdims=True),
         jnp.sum(ea * d, axis=1, keepdims=True),
     ]
-    lane = lax.broadcasted_iota(jnp.int32, (tokens, 128), 1)
-    packed = jnp.zeros((tokens, 128), F32)
+    lane = lax.broadcasted_iota(jnp.int32, (slots, 128), 1)
+    packed = jnp.zeros((slots, 128), F32)
     for i, figure in enumerate(figures):
         packed = jnp.where(lane == i, figure, packed)
-    packed = jnp.concatenate([packed, jnp.zeros((256 - tokens, 128), F32)], axis=0)
     st_a[k] = jnp.transpose(packed)[0:8, :]
     for m in range(1, 8):
         send(st_a.at[k], st_a.at[k], as_.at[m], ar.at[m], plane(m // 2, m % 2))
@@ -227,15 +262,20 @@
     divergence = mean_ratio - jnp.log(total) + jnp.log(full[3:4])
     offset = lse - lse_t + divergence
     cov = full[6:7] / total - mean_ratio * mean_logit
-    back = jnp.concatenate([lse, offset, divergence, cov, jnp.zeros((124, 256), F32)], axis=0)
-    back = jnp.transpose(back)[:tokens]
-    weight = weight_ref[...]
+    back = jnp.concatenate([lse, offset, divergence, cov, jnp.zeros((slots - 4, slots), F32)], axis=0)
+    back = jnp.transpose(back)
     loss_ref[...] = jnp.sum(weight * back[:, 2:3], axis=0, keepdims=True)
     prob = jnp.exp(s_log - back[:, 0:1])
     grad = ((weight * inv) * prob * (s_log - t_log - back[:, 1:2])).astype(BF16)
     g2[...] = grad
-    lane = lax.broadcasted_iota(jnp.int32, (tokens, 128), 1)
-    cols[...] = jnp.where(lane == 0, weight * inv * inv * back[:, 3:4] / DS, 0.0)
+    lane = lax.broadcasted_iota(jnp.int32, (slots, 128), 1)
+    figure = weight * inv * inv * back[:, 3:4] / DS
+    hi = figure.astype(BF16).astype(F32)
+    mid = (figure - hi).astype(BF16).astype(F32)
+    lo = figure - hi - mid
+    packed = jnp.where(lane == 0, hi, jnp.where(lane == 1, mid, jnp.where(lane == 2, lo, 0.0))).astype(BF16)
+    packed = lax.dot_general(pick_ref[...], packed, (((0,), (0,)), ((), ())), preferred_element_type=F32)
+    cols[...] = jnp.broadcast_to(jnp.sum(packed, axis=1, keepdims=True), cols.shape)
 
     def block_grad(at):
         return lax.dot_general(g2[...], wv[at], (((1,), (1,)), ((), ())), preferred_element_type=F32)
@@ -254,29 +294,20 @@
         else:
             own[...] = mine
 
-    head_copies = []
-    for i in range(8):
-        head[i] = lax.dot_general(
-            hg[i], g2[...], (((0,), (0,)), ((), ())), preferred_element_type=F32
-        ).astype(BF16)
-        copy = pltpu.make_async_copy(head.at[i], head_hbm.at[i], h_sem.at[i])
-        copy.start()
-        head_copies.append(copy)
-
     for vm in (1, 2, 3):
         arrived(r_x.at[vm], xs.at[vm], xr.at[vm], plane(vm, 0))
     total = own[...]
     for vm in (1, 2, 3):
         total = total + r_x[vm].astype(F32)
+    spread_out = lax.dot_general(
+        pick_ref[...], total.astype(BF16), (((0,), (0,)), ((), ())), preferred_element_type=F32
+    )
     for i in range(8):
-        rb[i] = total[i * rows:(i + 1) * rows].astype(BF16)
+        rb[i] = spread_out[i * rows:(i + 1) * rows].astype(BF16)
     for m in range(1, 8):
         send(rb.at[source(m)], rz.at[g], zs.at[m], zr.at[m], column(m // 2, m % 2))
     rz[g] = rb[g]
-    prod = total * s_blk[k, :tokens, :].astype(F32)
-    part = prod[0:8]
-    for i in range(1, tokens // 8):
-        part = part + prod[i * 8:(i + 1) * 8]
+    part = jnp.sum(total * jnp.where(slot_id < valid, s_blk[k].astype(F32), 0.0), axis=0, keepdims=True)
     gp[...] = part
     for m in range(1, 8):
         send(gp, gz.at[g], ys.at[m], yr.at[m], column(m // 2, m % 2))
@@ -298,11 +329,34 @@
         ng = gz[h]
         for i in range(1, 4):
             ng = ng + gz[2 * i + h]
-        gg_ref[:, at] = jnp.sum(ng, axis=0, keepdims=True)
-    for copy in head_copies:
-        copy.wait()
+        gg_ref[:, at] = ng
     for copy in sends:
         copy.wait_send()
+
+
+def head_kernel(
+    rows_hbm, grad_hbm, loss_hbm, hidden_hbm, gain_hbm, head_hbm, loss_out, hidden_out, gain_out,
+    rows_ref, grad_ref, head, in_sem, out_sem, pass_sem, grad_sem,
+):
+    copies = [pltpu.make_async_copy(grad_hbm, grad_ref, grad_sem)]
+    copies += [pltpu.make_async_copy(rows_hbm.at[i], rows_ref.at[i], in_sem.at[i]) for i in range(8)]
+    passed = [
+        pltpu.make_async_copy(src, dst, pass_sem.at[i])
+        for i, (src, dst) in enumerate(((hidden_hbm, hidden_out), (gain_hbm, gain_out), (loss_hbm, loss_out)))
+    ]
+    for copy in copies + passed:
+        copy.start()
+    copies[0].wait()
+    for i in range(8):
+        copies[i + 1].wait()
+        head[i] = lax.dot_general(
+            rows_ref[i], grad_ref[...], (((0,), (0,)), ((), ())), preferred_element_type=F32
+        ).astype(BF16)
+        copy = pltpu.make_async_copy(head.at[i], head_hbm.at[i], out_sem.at[i])
+        copy.start()
+        passed.append(copy)
+    for copy in passed:
+        copy.wait()
 
 
 def fused(
@@ -313,60 +367,78 @@
     tokens = rows * lax.axis_size("grp")
     voc = student_head.shape[1]
     half_s, half_t = wide_s // 2, wide_t // 2
-    positions = jnp.arange(SEQ, dtype=jnp.int32)
-    order = (episode_source[:, None] * SEQ + positions[None, :]).reshape(-1, 1)
-    valid = positions[None, :] < lengths[:, None]
-    weight = jnp.where(valid, 1.0 / lengths.astype(F32)[:, None], 0.0).reshape(-1, 1)
+    slots = -(-(tokens * 5 // 8 + 3) // 128) * 128
     vmem = pl.BlockSpec(memory_space=pltpu.VMEM)
-    hbm = pl.BlockSpec(memory_space=pl.ANY)
+    hbm = pl.BlockSpec(memory_space=pltpu.HBM)
     dma = pltpu.SemaphoreType.DMA
-    loss, grad_hidden, grad_gain, grad_head = pl.pallas_call(
+    loss, grad_hidden, grad_gain, scaled_rows, logit_grad = pl.pallas_call(
         kernel,
         out_shape=(
             jax.ShapeDtypeStruct((1, 1), F32),
             jax.ShapeDtypeStruct((rows, wide_s), BF16),
             jax.ShapeDtypeStruct((1, wide_s), F32),
-            jax.ShapeDtypeStruct((8, half_s, voc), BF16),
+            jax.ShapeDtypeStruct((8, slots, half_s), BF16),
+            jax.ShapeDtypeStruct((slots, voc), BF16),
         ),
-        in_specs=[vmem] * 5 + [hbm] * 2,
-        out_specs=(vmem, vmem, vmem, hbm),
+        in_specs=[hbm] * 7,
+        out_specs=(vmem,) * 5,
         scratch_shapes=[
             pltpu.VMEM((8, half_s, voc), BF16),
             pltpu.VMEM((8, half_t, voc), BF16),
-            pltpu.VMEM((2, rows, half_s), BF16),
-            pltpu.VMEM((2, rows, half_t), BF16),
+            pltpu.VMEM((rows, wide_s), BF16),
+            pltpu.VMEM((1, wide_s), F32),
+            pltpu.VMEM((1, episode_source.shape[0]), jnp.int32),
+            pltpu.VMEM((1, episode_source.shape[0]), jnp.int32),
+            pltpu.VMEM((slots, tokens), BF16),
             pltpu.VMEM((8, rows, half_s), BF16),
             pltpu.VMEM((8, rows, half_t), BF16),
-            pltpu.VMEM((8, tokens + 16, half_s), BF16),
-            pltpu.VMEM((8, tokens, half_t), BF16),
-            pltpu.VMEM((8, tokens, half_s), BF16),
-            pltpu.VMEM((tokens, voc), F32),
-            pltpu.VMEM((tokens, voc), F32),
+            pltpu.VMEM((8, slots, half_s), BF16),
+            pltpu.VMEM((8, slots, half_t), BF16),
+            pltpu.VMEM((slots, voc), F32),
+            pltpu.VMEM((slots, voc), F32),
+            pltpu.VMEM((slots, 128), F32),
             pltpu.VMEM((tokens, 128), F32),
-            pltpu.VMEM((tokens, 128), F32),
-            pltpu.VMEM((8, 8, 256), F32),
-            pltpu.VMEM((4, 8, 256), F32),
-            pltpu.VMEM((tokens, voc), BF16),
-            pltpu.VMEM((tokens, half_s), F32),
-            pltpu.VMEM((4, tokens, half_s), BF16),
-            pltpu.VMEM((4, tokens, half_s), BF16),
-            pltpu.VMEM((4, tokens, half_s), BF16),
-            pltpu.VMEM((4, tokens, half_s), BF16),
+            pltpu.VMEM((8, 8, slots), F32),
+            pltpu.VMEM((4, 8, slots), F32),
+            pltpu.VMEM((slots, half_s), F32),
+            pltpu.VMEM((4, slots, half_s), BF16),
+            pltpu.VMEM((4, slots, half_s), BF16),
+            pltpu.VMEM((4, slots, half_s), BF16),
+            pltpu.VMEM((4, slots, half_s), BF16),
             pltpu.VMEM((8, rows, half_s), BF16),
             pltpu.VMEM((8, rows, half_s), BF16),
-            pltpu.VMEM((8, half_s), F32),
-            pltpu.VMEM((8, 8, half_s), F32),
-            pltpu.VMEM((8, half_s, voc), BF16),
+            pltpu.VMEM((1, half_s), F32),
+            pltpu.VMEM((8, 1, half_s), F32),
             dma(()), dma(()), dma((8,)),
         ] + [dma((8,))] * 20,
         compiler_params=pltpu.CompilerParams(
-            collective_id=0, has_side_effects=True, vmem_limit_bytes=52 * 1024 * 1024
+            collective_id=0, has_side_effects=True, vmem_limit_bytes=LIMIT * 1024
         ),
         cost_estimate=pl.CostEstimate(flops=2600000000, bytes_accessed=11000000, transcendentals=400000),
     )(
-        student_hidden, teacher_hidden, norm_gain.reshape(1, -1), order, weight,
+        student_hidden, teacher_hidden, norm_gain.reshape(1, -1),
+        episode_source.reshape(1, -1), lengths.reshape(1, -1),
         student_head.reshape(8, half_s, voc), teacher_head.reshape(8, half_t, voc),
     )
+    grad_head, loss, grad_hidden, grad_gain = pl.pallas_call(
+        head_kernel,
+        out_shape=(
+            jax.ShapeDtypeStruct((8, half_s, voc), BF16),
+            jax.ShapeDtypeStruct((1, 1), F32),
+            jax.ShapeDtypeStruct((rows, wide_s), BF16),
+            jax.ShapeDtypeStruct((1, wide_s), F32),
+        ),
+        in_specs=[hbm] * 5,
+        out_specs=(hbm,) * 4,
+        scratch_shapes=[
+            pltpu.VMEM((8, slots, half_s), BF16),
+            pltpu.VMEM((slots, voc), BF16),
+            pltpu.VMEM((8, half_s, voc), BF16),
+            dma((8,)), dma((8,)), dma((3,)), dma(()),
+        ],
+        compiler_params=pltpu.CompilerParams(vmem_limit_bytes=LIMIT * 1024),
+        cost_estimate=pl.CostEstimate(flops=402653184, bytes_accessed=4300000, transcendentals=0),
+    )(scaled_rows, logit_grad, loss, grad_hidden, grad_gain)
     return (loss[0, 0], grad_hidden, grad_gain.reshape(-1), grad_head.reshape(student_head.shape))
 
 

time: 79.5 us -> 61.8 us (0.78)
  local copies, waits for them, and re-layouts: 7.57 us -> 0 us
  Pallas kernels: 67.1 us -> 61 us
  other arithmetic: 2.13 us -> 0 us
  between operations: 2.33 us -> 0.64 us
    pallas_call x1, Pallas kernels: 67.1 us -> 55.7 us  [fused(): pl.pallas_call(kernel, out_shape=(jax.ShapeDtypeStruct((1, 1), F32), jax....]
    unnamed x9 -> x0, local copies, waits for them, and re-layouts: 7.41 us -> none
    pallas_call x0 -> x1, Pallas kernels: none -> 5.33 us  [fused(): pl.pallas_call(head_kernel, out_shape=(jax.ShapeDtypeStruct((8, half_s, v...]
where the time goes in v2:
time: 61.8 us; the launch traced here: 61.6 us
  Pallas kernels  61 us (99%)
  between operations  0.64 us (1%)
    pallas_call x1, Pallas kernels, fused(): pl.pallas_call(kernel, out_shape=(jax.ShapeDtypeStruct((1, 1), F32), jax....  55.7 us
    pallas_call x1, Pallas kernels, fused(): pl.pallas_call(head_kernel, out_shape=(jax.ShapeDtypeStruct((8, half_s, v...  5.33 us

profile of v2, /device:TPU:0, one launch (start us, length us, event | category | flops | bytes accessed | tf_op | source)
XLA Modules:
  0.0 61.6 jit_solution(2545879663473784542)
XLA Ops:
  0.6 55.7 %shard_map.102 = (f32[1,1]{1,0:T(1,128)}, bf16[24,1024]{1,0:T(8,128)(2,1)}, f32[1,1024]{1,0:T(1,128)}, bf16[8,128,512]{2,1,0:T(8,128)(2,1)}, bf16[128,384]{1,0:T(8,128)(2,1)}) custom-call(bf16[24,1024]{1,0:T(8,128)(2,1)} %sh_hbm.1, bf16[24,1280]{1,0:T(8,128)(2,1)} %th_hbm.1, f32[1,1024]{1,0:T(1,128)} %bitcast.10, s32[1,96]{1,0:T(1,128)} %bitcast.11, ...), custom_call_target="tpu_custom_call" | custom-call | flops 2600000000 | bytes 11000000 | tf_op jit(solution)/shard_map/pallas_call | solution.py:374
  56.3 5.3 %shard_map.103 = (bf16[8,512,384]{2,1,0:T(8,128)(2,1)}, f32[1,1]{1,0:T(1,128)}, bf16[24,1024]{1,0:T(8,128)(2,1)}, f32[1,1024]{1,0:T(1,128)}) custom-call(bf16[8,128,512]{2,1,0:T(8,128)(2,1)} %get-tuple-element.13.rows_hbm, bf16[128,384]{1,0:T(8,128)(2,1)} %get-tuple-element.14.grad_hbm, f32[1,1]{1,0:T(1,128)} %get-tuple-element.15.loss_hbm, ...), custom_call_target="tpu_custom_call" | custom-call | flops 402653184 | bytes 4300000 | tf_op jit(solution)/shard_map/pallas_call | solution.py:423

commit v3 on v2

--- a/solution.py
+++ b/solution.py
@@ -49,10 +49,10 @@
 
 def kernel(
     sh_hbm, th_hbm, gain_hbm, source_hbm, lengths_hbm, w_hbm, t_hbm,
-    loss_ref, gh_ref, gg_ref, hg, g2,
-    wv, tv, sh_ref, gain_ref, source_ref, lengths_ref, pick_ref, in_s, in_t, s_blk, t_blk, s_acc, t_acc, sq, cols,
-    st_a, st_b, own, p_sib, r_sib, p_x, r_x, rb, rz, gp, gz,
-    w_sem, t_sem, l_sem, s1s, s1r, t1s, t1r, s2s, s2r, t2s, t2r, as_, ar, bs, br,
+    loss_ref, gh_ref, gg_ref, head_hbm,
+    wv, tv, sh_ref, gain_ref, source_ref, lengths_ref, pick_ref, in_s, in_t, s_blk, t_blk, hg, s_acc, t_acc, sq, cols,
+    st_a, st_b, g2, own, p_sib, r_sib, p_x, r_x, rb, rz, gp, gz, head,
+    w_sem, t_sem, h_sem, l_sem, s1s, s1r, t1s, t1r, s2s, s2r, t2s, t2r, as_, ar, bs, br,
     qs, qr, xs, xr, zs, zr, ys, yr,
 ):
     g = lax.axis_index("grp")
@@ -192,9 +192,9 @@
         for i in range(1, half_s // 128):
             partial = partial + squares[:, i * 128:(i + 1) * 128]
         sq[...] += partial
-        scaled = (x * scale).astype(BF16)
-        hg[at] = scaled
-        s_acc[...] += jnp.dot(scaled, wv[at], preferred_element_type=F32)
+        scaled = x * scale
+        hg[at] = jnp.transpose(scaled).astype(BF16)
+        s_acc[...] += jnp.dot(scaled.astype(BF16), wv[at], preferred_element_type=F32)
 
     def teacher_block(at):
         t_acc[...] += jnp.dot(t_blk[at], tv[at], preferred_element_type=F32)
@@ -281,6 +281,7 @@
         return lax.dot_general(g2[...], wv[at], (((1,), (1,)), ((), ())), preferred_element_type=F32)
 
     order = (1, 2, 3, 0)
+    part = half_s // 2
     for vm in order:
         p_sib[vm] = block_grad(slot(vm, 1)).astype(BF16)
         send(p_sib.at[vm], r_sib.at[vm], qs.at[vm], qr.at[vm], plane(0, 1))
@@ -290,30 +291,52 @@
         mine = mine + r_sib[vm].astype(F32)
         if vm:
             p_x[vm] = mine.astype(BF16)
-            send(p_x.at[vm], r_x.at[vm], xs.at[vm], xr.at[vm], plane(vm, 0))
+            send(p_x.at[vm, :, 0:part], r_x.at[vm, :, 0:part], xs.at[vm], xr.at[vm], plane(vm, 0))
         else:
             own[...] = mine
-
     for vm in (1, 2, 3):
-        arrived(r_x.at[vm], xs.at[vm], xr.at[vm], plane(vm, 0))
-    total = own[...]
-    for vm in (1, 2, 3):
-        total = total + r_x[vm].astype(F32)
-    spread_out = lax.dot_general(
-        pick_ref[...], total.astype(BF16), (((0,), (0,)), ((), ())), preferred_element_type=F32
-    )
-    for i in range(8):
-        rb[i] = spread_out[i * rows:(i + 1) * rows].astype(BF16)
-    for m in range(1, 8):
-        send(rb.at[source(m)], rz.at[g], zs.at[m], zr.at[m], column(m // 2, m % 2))
+        send(p_x.at[vm, :, part:], r_x.at[vm, :, part:], xs.at[vm + 4], xr.at[vm + 4], plane(vm, 0))
+
+    def head_block(i):
+        head[i] = jnp.dot(hg[i], g2[...], preferred_element_type=F32).astype(BF16)
+        copy = pltpu.make_async_copy(head.at[i], head_hbm.at[i], h_sem.at[i])
+        copy.start()
+        head_copies.append(copy)
+
+    head_copies = []
+    for i in range(4):
+        head_block(i)
+    for h in range(2):
+        at = slice(h * part, (h + 1) * part)
+        for vm in (1, 2, 3):
+            arrived(r_x.at[vm, :, at], xs.at[vm + 4 * h], xr.at[vm + 4 * h], plane(vm, 0))
+        total = own[:, at]
+        for vm in (1, 2, 3):
+            total = total + r_x[vm, :, at].astype(F32)
+        spread_out = lax.dot_general(
+            pick_ref[...], total.astype(BF16), (((0,), (0,)), ((), ())), preferred_element_type=F32
+        )
+        for i in range(8):
+            rb[i, :, at] = spread_out[i * rows:(i + 1) * rows].astype(BF16)
+        for m in range(1, 8):
+            send(
+                rb.at[source(m), :, at], rz.at[g, :, at], zs.at[m + 8 * h], zr.at[m + 8 * h],
+                column(m // 2, m % 2),
+            )
+        gp[:, at] = jnp.sum(
+            total * jnp.where(slot_id < valid, s_blk[k].astype(F32), 0.0)[:, at], axis=0, keepdims=True
+        )
+        if h:
+            for m in range(1, 8):
+                send(gp, gz.at[g], ys.at[m], yr.at[m], column(m // 2, m % 2))
+        for i in range(4 + 2 * h, 6 + 2 * h):
+            head_block(i)
     rz[g] = rb[g]
-    part = jnp.sum(total * jnp.where(slot_id < valid, s_blk[k].astype(F32), 0.0), axis=0, keepdims=True)
-    gp[...] = part
-    for m in range(1, 8):
-        send(gp, gz.at[g], ys.at[m], yr.at[m], column(m // 2, m % 2))
-    gz[g] = part
-    for m in range(1, 8):
-        arrived(rz.at[source(m)], zs.at[m], zr.at[m], column(m // 2, m % 2))
+    gz[g] = gp[...]
+    for h in range(2):
+        at = slice(h * part, (h + 1) * part)
+        for m in range(1, 8):
+            arrived(rz.at[source(m), :, at], zs.at[m + 8 * h], zr.at[m + 8 * h], column(m // 2, m % 2))
     own_cols = cols[pl.ds(pl.multiple_of(g * rows, 8), rows), :][:, 0:1]
     for h in range(2):
         at = slice(h * half_s, (h + 1) * half_s)
@@ -330,32 +353,26 @@
         for i in range(1, 4):
             ng = ng + gz[2 * i + h]
         gg_ref[:, at] = ng
+    for copy in head_copies:
+        copy.wait()
     for copy in sends:
         copy.wait_send()
 
 
-def head_kernel(
-    rows_hbm, grad_hbm, loss_hbm, hidden_hbm, gain_hbm, head_hbm, loss_out, hidden_out, gain_out,
-    rows_ref, grad_ref, head, in_sem, out_sem, pass_sem, grad_sem,
+def finish(
+    head_in, loss_in, hidden_in, gain_in, head_out, loss_out, hidden_out, gain_out,
+    head, hidden, gain, loss, in_sem, out_sem,
 ):
-    copies = [pltpu.make_async_copy(grad_hbm, grad_ref, grad_sem)]
-    copies += [pltpu.make_async_copy(rows_hbm.at[i], rows_ref.at[i], in_sem.at[i]) for i in range(8)]
-    passed = [
-        pltpu.make_async_copy(src, dst, pass_sem.at[i])
-        for i, (src, dst) in enumerate(((hidden_hbm, hidden_out), (gain_hbm, gain_out), (loss_hbm, loss_out)))
-    ]
-    for copy in copies + passed:
+    moves = [(head_in.at[i], head.at[i], head_out.at[i]) for i in range(8)]
+    moves += [(hidden_in, hidden, hidden_out), (gain_in, gain, gain_out), (loss_in, loss, loss_out)]
+    inward = [pltpu.make_async_copy(a, b, in_sem.at[i]) for i, (a, b, _) in enumerate(moves)]
+    outward = [pltpu.make_async_copy(b, c, out_sem.at[i]) for i, (_, b, c) in enumerate(moves)]
+    for copy in inward:
         copy.start()
-    copies[0].wait()
-    for i in range(8):
-        copies[i + 1].wait()
-        head[i] = lax.dot_general(
-            rows_ref[i], grad_ref[...], (((0,), (0,)), ((), ())), preferred_element_type=F32
-        ).astype(BF16)
-        copy = pltpu.make_async_copy(head.at[i], head_hbm.at[i], out_sem.at[i])
-        copy.start()
-        passed.append(copy)
-    for copy in passed:
+    for first, second in zip(inward, outward):
+        first.wait()
+        second.start()
+    for copy in outward:
         copy.wait()
 
 
@@ -371,17 +388,16 @@
     vmem = pl.BlockSpec(memory_space=pltpu.VMEM)
     hbm = pl.BlockSpec(memory_space=pltpu.HBM)
     dma = pltpu.SemaphoreType.DMA
-    loss, grad_hidden, grad_gain, scaled_rows, logit_grad = pl.pallas_call(
+    loss, grad_hidden, grad_gain, grad_head = pl.pallas_call(
         kernel,
         out_shape=(
             jax.ShapeDtypeStruct((1, 1), F32),
             jax.ShapeDtypeStruct((rows, wide_s), BF16),
             jax.ShapeDtypeStruct((1, wide_s), F32),
-            jax.ShapeDtypeStruct((8, slots, half_s), BF16),
-            jax.ShapeDtypeStruct((slots, voc), BF16),
+            jax.ShapeDtypeStruct((8, half_s, voc), BF16),
         ),
         in_specs=[hbm] * 7,
-        out_specs=(vmem,) * 5,
+        out_specs=(vmem, vmem, vmem, hbm),
         scratch_shapes=[
             pltpu.VMEM((8, half_s, voc), BF16),
             pltpu.VMEM((8, half_t, voc), BF16),
@@ -394,12 +410,14 @@
             pltpu.VMEM((8, rows, half_t), BF16),
             pltpu.VMEM((8, slots, half_s), BF16),
             pltpu.VMEM((8, slots, half_t), BF16),
+            pltpu.VMEM((8, half_s, slots), BF16),
             pltpu.VMEM((slots, voc), F32),
             pltpu.VMEM((slots, voc), F32),
             pltpu.VMEM((slots, 128), F32),
             pltpu.VMEM((tokens, 128), F32),
             pltpu.VMEM((8, 8, slots), F32),
             pltpu.VMEM((4, 8, slots), F32),
+            pltpu.VMEM((slots, voc), BF16),
             pltpu.VMEM((slots, half_s), F32),
             pltpu.VMEM((4, slots, half_s), BF16),
             pltpu.VMEM((4, slots, half_s), BF16),
@@ -409,8 +427,9 @@
             pltpu.VMEM((8, rows, half_s), BF16),
             pltpu.VMEM((1, half_s), F32),
             pltpu.VMEM((8, 1, half_s), F32),
-            dma(()), dma(()), dma((8,)),
-        ] + [dma((8,))] * 20,
+            pltpu.VMEM((8, half_s, voc), BF16),
+            dma(()), dma(()), dma((8,)), dma((8,)),
+        ] + [dma((8,))] * 16 + [dma((16,))] * 2 + [dma((8,))] * 2,
         compiler_params=pltpu.CompilerParams(
             collective_id=0, has_side_effects=True, vmem_limit_bytes=LIMIT * 1024
         ),
@@ -420,25 +439,22 @@
         episode_source.reshape(1, -1), lengths.reshape(1, -1),
         student_head.reshape(8, half_s, voc), teacher_head.reshape(8, half_t, voc),
     )
+    results = (grad_head, loss, grad_hidden, grad_gain)
     grad_head, loss, grad_hidden, grad_gain = pl.pallas_call(
-        head_kernel,
-        out_shape=(
-            jax.ShapeDtypeStruct((8, half_s, voc), BF16),
-            jax.ShapeDtypeStruct((1, 1), F32),
-            jax.ShapeDtypeStruct((rows, wide_s), BF16),
-            jax.ShapeDtypeStruct((1, wide_s), F32),
-        ),
-        in_specs=[hbm] * 5,
+        finish,
+        out_shape=tuple(jax.ShapeDtypeStruct(r.shape, r.dtype) for r in results),
+        in_specs=[hbm] * 4,
         out_specs=(hbm,) * 4,
         scratch_shapes=[
-            pltpu.VMEM((8, slots, half_s), BF16),
-            pltpu.VMEM((slots, voc), BF16),
             pltpu.VMEM((8, half_s, voc), BF16),
-            dma((8,)), dma((8,)), dma((3,)), dma(()),
+            pltpu.VMEM((rows, wide_s), BF16),
+            pltpu.VMEM((1, wide_s), F32),
+            pltpu.VMEM((1, 1), F32),
+            dma((11,)), dma((11,)),
         ],
         compiler_params=pltpu.CompilerParams(vmem_limit_bytes=LIMIT * 1024),
-        cost_estimate=pl.CostEstimate(flops=402653184, bytes_accessed=4300000, transcendentals=0),
-    )(scaled_rows, logit_grad, loss, grad_hidden, grad_gain)
+        cost_estimate=pl.CostEstimate(flops=0, bytes_accessed=6400000, transcendentals=0),
+    )(*results)
     return (loss[0, 0], grad_hidden, grad_gain.reshape(-1), grad_head.reshape(student_head.shape))
 
 

time: 61.8 us -> 57.9 us (0.937)
  Pallas kernels: 61 us -> 57.1 us
    pallas_call x1, Pallas kernels: 55.7 us -> 53.6 us  [fused(): pl.pallas_call(kernel, out_shape=(jax.ShapeDtypeStruct((1, 1), F32), jax....]
    pallas_call x1, Pallas kernels: 5.33 us -> 3.52 us  [fused(): pl.pallas_call(finish, out_shape=tuple((jax.ShapeDtypeStruct(r.shape, r.d...]
where the time goes in v3:
time: 57.9 us; the launch traced here: 57.8 us
  Pallas kernels  57.1 us (99%)
  between operations  0.64 us (1%)
    pallas_call x1, Pallas kernels, fused(): pl.pallas_call(kernel, out_shape=(jax.ShapeDtypeStruct((1, 1), F32), jax....  53.6 us
    pallas_call x1, Pallas kernels, fused(): pl.pallas_call(finish, out_shape=tuple((jax.ShapeDtypeStruct(r.shape, r.d...  3.52 us

profile of v3, /device:TPU:0, one launch (start us, length us, event | category | flops | bytes accessed | tf_op | source)
XLA Modules:
  0.0 57.8 jit_solution(9300273900302062922)
XLA Ops:
  0.6 53.6 %shard_map.102 = (f32[1,1]{1,0:T(1,128)}, bf16[24,1024]{1,0:T(8,128)(2,1)}, f32[1,1024]{1,0:T(1,128)}, bf16[8,512,384]{2,1,0:T(8,128)(2,1)}) custom-call(bf16[24,1024]{1,0:T(8,128)(2,1)} %sh_hbm.1, bf16[24,1280]{1,0:T(8,128)(2,1)} %th_hbm.1, f32[1,1024]{1,0:T(1,128)} %bitcast.11, s32[1,96]{1,0:T(1,128)} %bitcast.13, s32[1,96]{1,0:T(1,128)} %bitcast.14, ...), custom_call_target="tpu_custom_call" | custom-call | flops 2600000000 | bytes 11000000 | tf_op jit(solution)/shard_map/pallas_call | solution.py:391
  54.3 3.5 %shard_map.103 = (bf16[8,512,384]{2,1,0:T(8,128)(2,1)}, f32[1,1]{1,0:T(1,128)}, bf16[24,1024]{1,0:T(8,128)(2,1)}, f32[1,1024]{1,0:T(1,128)}) custom-call(bf16[8,512,384]{2,1,0:T(8,128)(2,1)} %get-tuple-element.12.head_in, f32[1,1]{1,0:T(1,128)} %get-tuple-element.13.loss_in, bf16[24,1024]{1,0:T(8,128)(2,1)} %get-tuple-element.14.hidden_in, ...), custom_call_target="tpu_custom_call" | custom-call | bytes 6400000 | tf_op jit(solution)/shard_map/pallas_call | solution.py:443

commit v4 on v3

--- a/solution.py
+++ b/solution.py
@@ -160,6 +160,33 @@
     def source(m):
         return flip(z, m // 2) * 2 + (1 - c if m % 2 else c)
 
+    halves = (slice(0, slots // 2), slice(slots // 2, slots))
+
+    def share(blk, ssem, rsem):
+        for vm, half_id in ((1, 0), (2, 1), (1, 1), (2, 0)):
+            piece = blk.at[k, halves[half_id]]
+            send(piece, piece, ssem.at[vm * 4 + half_id], rsem.at[vm * 4 + half_id], plane(vm, 0))
+        send(blk.at[k], blk.at[k], ssem.at[2], rsem.at[2], plane(0, 1))
+
+    def landed(blk, ssem, rsem, vm, half_id):
+        piece = blk.at[slot(vm, 0), halves[half_id]]
+        arrived(piece, ssem.at[vm * 4 + half_id], rsem.at[vm * 4 + half_id], plane(vm, 0))
+        return piece
+
+    def relay(blk, ssem, rsem):
+        for vm, half_id in ((1, 0), (2, 1)):
+            piece = landed(blk, ssem, rsem, vm, half_id)
+            send(piece, piece, ssem.at[12 + half_id], rsem.at[12 + half_id], plane(3 - vm, 0))
+
+    def to_sibling(blk, ssem, rsem, vm):
+        for half_id in {1: (1,), 2: (0,), 3: (0, 1)}[vm]:
+            landed(blk, ssem, rsem, vm, half_id)
+        at = slot(vm, 0)
+        send(blk.at[at], blk.at[at], ssem.at[vm * 4 + 2], rsem.at[vm * 4 + 2], plane(0, 1))
+
+    def sibling(blk, ssem, rsem, vm):
+        arrived(blk.at[slot(vm, 1)], ssem.at[vm * 4 + 2], rsem.at[vm * 4 + 2], plane(0, 1))
+
     for m in range(1, 8):
         arrived(in_s.at[source(m)], s1s.at[m], s1r.at[m], column(m // 2, m % 2))
     for copy in local_copies[3:]:
@@ -167,21 +194,10 @@
     block = jnp.concatenate([in_s[i].astype(F32) for i in range(8)], axis=0).astype(BF16)
     block = jnp.dot(pick, block, preferred_element_type=F32)
     s_blk[k] = jnp.where(slot_id < valid, block, gain_rows).astype(BF16)
-    for vm in (1, 2, 3):
-        send(s_blk.at[k], s_blk.at[k], s2s.at[vm * 2], s2r.at[vm * 2], plane(vm, 0))
-    send(s_blk.at[k], s_blk.at[k], s2s.at[1], s2r.at[1], plane(0, 1))
-    for m in range(1, 8):
-        arrived(in_t.at[source(m)], t1s.at[m], t1r.at[m], column(m // 2, m % 2))
-    block = jnp.concatenate([in_t[i].astype(F32) for i in range(8)], axis=0).astype(BF16)
-    t_blk[k] = jnp.dot(pick_t, block, preferred_element_type=F32).astype(BF16)
-    for vm in (1, 2, 3):
-        send(t_blk.at[k], t_blk.at[k], t2s.at[vm * 2], t2r.at[vm * 2], plane(vm, 0))
-    send(t_blk.at[k], t_blk.at[k], t2s.at[1], t2r.at[1], plane(0, 1))
-
+    share(s_blk, s2s, s2r)
     s_acc[...] = jnp.zeros_like(s_acc)
     t_acc[...] = jnp.zeros_like(t_acc)
     sq[...] = jnp.zeros_like(sq)
-    w_copy.wait()
 
     def student_block(at):
         x = s_blk[at].astype(F32)
@@ -199,31 +215,45 @@
     def teacher_block(at):
         t_acc[...] += jnp.dot(t_blk[at], tv[at], preferred_element_type=F32)
 
-    def relay(blk, ssem, rsem, vm):
-        at = slot(vm, 0)
-        arrived(blk.at[at], ssem.at[vm * 2], rsem.at[vm * 2], plane(vm, 0))
-        send(blk.at[at], blk.at[at], ssem.at[vm * 2 + 1], rsem.at[vm * 2 + 1], plane(0, 1))
-
-    def sibling(blk, ssem, rsem, vm):
-        arrived(blk.at[slot(vm, 1)], ssem.at[vm * 2 + 1], rsem.at[vm * 2 + 1], plane(0, 1))
-
+    w_copy.wait()
     student_block(k)
+    sibling(s_blk, s2s, s2r, 0)
+    student_block(slot(0, 1))
+    relay(s_blk, s2s, s2r)
+    for m in range(1, 8):
+        arrived(in_t.at[source(m)], t1s.at[m], t1r.at[m], column(m // 2, m % 2))
+    block = jnp.concatenate([in_t[i].astype(F32) for i in range(8)], axis=0).astype(BF16)
+    t_blk[k] = jnp.dot(pick_t, block, preferred_element_type=F32).astype(BF16)
+    share(t_blk, t2s, t2r)
+
+    to_sibling(s_blk, s2s, s2r, 1)
+    to_sibling(s_blk, s2s, s2r, 2)
     t_copy.wait()
     teacher_block(k)
-    sibling(s_blk, s2s, s2r, 0)
-    student_block(slot(0, 1))
+    student_block(slot(1, 0))
+    student_block(slot(2, 0))
+    relay(t_blk, t2s, t2r)
+    sibling(s_blk, s2s, s2r, 1)
+    student_block(slot(1, 1))
+    sibling(s_blk, s2s, s2r, 2)
+    student_block(slot(2, 1))
+    to_sibling(s_blk, s2s, s2r, 3)
+    student_block(slot(3, 0))
     sibling(t_blk, t2s, t2r, 0)
     teacher_block(slot(0, 1))
-    for vm in (1, 2, 3):
-        relay(s_blk, s2s, s2r, vm)
-        student_block(slot(vm, 0))
-        sibling(s_blk, s2s, s2r, vm)
-        student_block(slot(vm, 1))
-    for vm in (1, 2, 3):
-        relay(t_blk, t2s, t2r, vm)
-        teacher_block(slot(vm, 0))
+    to_sibling(t_blk, t2s, t2r, 1)
+    to_sibling(t_blk, t2s, t2r, 2)
+    sibling(s_blk, s2s, s2r, 3)
+    student_block(slot(3, 1))
+    teacher_block(slot(1, 0))
+    teacher_block(slot(2, 0))
+    for vm in (1, 2):
         sibling(t_blk, t2s, t2r, vm)
         teacher_block(slot(vm, 1))
+    to_sibling(t_blk, t2s, t2r, 3)
+    teacher_block(slot(3, 0))
+    sibling(t_blk, t2s, t2r, 3)
+    teacher_block(slot(3, 1))
 
     inv = lax.rsqrt(jnp.sum(sq[...], axis=1, keepdims=True) / DS + EPSILON)
     s_log = s_acc[...] * inv
@@ -264,18 +294,9 @@
     cov = full[6:7] / total - mean_ratio * mean_logit
     back = jnp.concatenate([lse, offset, divergence, cov, jnp.zeros((slots - 4, slots), F32)], axis=0)
     back = jnp.transpose(back)
-    loss_ref[...] = jnp.sum(weight * back[:, 2:3], axis=0, keepdims=True)
     prob = jnp.exp(s_log - back[:, 0:1])
     grad = ((weight * inv) * prob * (s_log - t_log - back[:, 1:2])).astype(BF16)
     g2[...] = grad
-    lane = lax.broadcasted_iota(jnp.int32, (slots, 128), 1)
-    figure = weight * inv * inv * back[:, 3:4] / DS
-    hi = figure.astype(BF16).astype(F32)
-    mid = (figure - hi).astype(BF16).astype(F32)
-    lo = figure - hi - mid
-    packed = jnp.where(lane == 0, hi, jnp.where(lane == 1, mid, jnp.where(lane == 2, lo, 0.0))).astype(BF16)
-    packed = lax.dot_general(pick_ref[...], packed, (((0,), (0,)), ((), ())), preferred_element_type=F32)
-    cols[...] = jnp.broadcast_to(jnp.sum(packed, axis=1, keepdims=True), cols.shape)
 
     def block_grad(at):
         return lax.dot_general(g2[...], wv[at], (((1,), (1,)), ((), ())), preferred_element_type=F32)
@@ -296,6 +317,16 @@
             own[...] = mine
     for vm in (1, 2, 3):
         send(p_x.at[vm, :, part:], r_x.at[vm, :, part:], xs.at[vm + 4], xr.at[vm + 4], plane(vm, 0))
+
+    loss_ref[...] = jnp.sum(weight * back[:, 2:3], axis=0, keepdims=True)
+    lane = lax.broadcasted_iota(jnp.int32, (slots, 128), 1)
+    figure = weight * inv * inv * back[:, 3:4] / DS
+    hi = figure.astype(BF16).astype(F32)
+    mid = (figure - hi).astype(BF16).astype(F32)
+    lo = figure - hi - mid
+    packed = jnp.where(lane == 0, hi, jnp.where(lane == 1, mid, jnp.where(lane == 2, lo, 0.0))).astype(BF16)
+    packed = lax.dot_general(pick_ref[...], packed, (((0,), (0,)), ((), ())), preferred_element_type=F32)
+    cols[...] = jnp.broadcast_to(jnp.sum(packed, axis=1, keepdims=True), cols.shape)
 
     def head_block(i):
         head[i] = jnp.dot(hg[i], g2[...], preferred_element_type=F32).astype(BF16)
@@ -429,7 +460,7 @@
             pltpu.VMEM((8, 1, half_s), F32),
             pltpu.VMEM((8, half_s, voc), BF16),
             dma(()), dma(()), dma((8,)), dma((8,)),
-        ] + [dma((8,))] * 16 + [dma((16,))] * 2 + [dma((8,))] * 2,
+        ] + [dma((8,))] * 4 + [dma((16,))] * 4 + [dma((8,))] * 8 + [dma((16,))] * 2 + [dma((8,))] * 2,
         compiler_params=pltpu.CompilerParams(
             collective_id=0, has_side_effects=True, vmem_limit_bytes=LIMIT * 1024
         ),

time: 57.9 us -> 54.8 us (0.946)
  Pallas kernels: 57.1 us -> 54 us
    pallas_call x1, Pallas kernels: 53.6 us -> 50.4 us  [fused(): pl.pallas_call(kernel, out_shape=(jax.ShapeDtypeStruct((1, 1), F32), jax....]
where the time goes in v4:
time: 54.8 us; the launch traced here: 54.6 us
  Pallas kernels  54 us (99%)
  between operations  0.64 us (1%)
    pallas_call x1, Pallas kernels, fused(): pl.pallas_call(kernel, out_shape=(jax.ShapeDtypeStruct((1, 1), F32), jax....  50.4 us
    pallas_call x1, Pallas kernels, fused(): pl.pallas_call(finish, out_shape=tuple((jax.ShapeDtypeStruct(r.shape, r.d...  3.52 us

profile of v4, /device:TPU:0, one launch (start us, length us, event | category | flops | bytes accessed | tf_op | source)
XLA Modules:
  0.0 54.6 jit_solution(9215974527088277567)
XLA Ops:
  0.6 50.4 %shard_map.102 = (f32[1,1]{1,0:T(1,128)}, bf16[24,1024]{1,0:T(8,128)(2,1)}, f32[1,1024]{1,0:T(1,128)}, bf16[8,512,384]{2,1,0:T(8,128)(2,1)}) custom-call(bf16[24,1024]{1,0:T(8,128)(2,1)} %sh_hbm.1, bf16[24,1280]{1,0:T(8,128)(2,1)} %th_hbm.1, f32[1,1024]{1,0:T(1,128)} %bitcast.11, s32[1,96]{1,0:T(1,128)} %bitcast.13, s32[1,96]{1,0:T(1,128)} %bitcast.14, ...), custom_call_target="tpu_custom_call" | custom-call | flops 2600000000 | bytes 11000000 | tf_op jit(solution)/shard_map/pallas_call | solution.py:422
  51.1 3.5 %shard_map.103 = (bf16[8,512,384]{2,1,0:T(8,128)(2,1)}, f32[1,1]{1,0:T(1,128)}, bf16[24,1024]{1,0:T(8,128)(2,1)}, f32[1,1024]{1,0:T(1,128)}) custom-call(bf16[8,512,384]{2,1,0:T(8,128)(2,1)} %get-tuple-element.12.head_in, f32[1,1]{1,0:T(1,128)} %get-tuple-element.13.loss_in, bf16[24,1024]{1,0:T(8,128)(2,1)} %get-tuple-element.14.hidden_in, ...), custom_call_target="tpu_custom_call" | custom-call | bytes 6400000 | tf_op jit(solution)/shard_map/pallas_call | solution.py:474

commit v5 on v4

--- a/solution.py
+++ b/solution.py
@@ -50,7 +50,7 @@
 def kernel(
     sh_hbm, th_hbm, gain_hbm, source_hbm, lengths_hbm, w_hbm, t_hbm,
     loss_ref, gh_ref, gg_ref, head_hbm,
-    wv, tv, sh_ref, gain_ref, source_ref, lengths_ref, pick_ref, in_s, in_t, s_blk, t_blk, hg, s_acc, t_acc, sq, cols,
+    wv, tv, sh_ref, gain_ref, source_ref, lengths_ref, pick_ref, in_s, in_t, s_blk, t_blk, hg, s_acc, t_acc, raw, cols,
     st_a, st_b, g2, own, p_sib, r_sib, p_x, r_x, rb, rz, gp, gz, head,
     w_sem, t_sem, h_sem, l_sem, s1s, s1r, t1s, t1r, s2s, s2r, t2s, t2r, as_, ar, bs, br,
     qs, qr, xs, xr, zs, zr, ys, yr,
@@ -149,13 +149,7 @@
 
     gain = gain_ref[...]
     own_gain = jnp.where(c == 0, gain[:, :half_s], gain[:, half_s:])
-    hi = own_gain.astype(BF16).astype(F32)
-    mid = (own_gain - hi).astype(BF16).astype(F32)
-    lo = own_gain - hi - mid
     slot_id = lax.broadcasted_iota(jnp.int32, (slots, half_s), 0)
-    gain_rows = jnp.where(
-        slot_id == valid, hi, jnp.where(slot_id == valid + 1, mid, jnp.where(slot_id == valid + 2, lo, 0.0))
-    )
 
     def source(m):
         return flip(z, m // 2) * 2 + (1 - c if m % 2 else c)
@@ -193,24 +187,26 @@
         copy.wait()
     block = jnp.concatenate([in_s[i].astype(F32) for i in range(8)], axis=0).astype(BF16)
     block = jnp.dot(pick, block, preferred_element_type=F32)
-    s_blk[k] = jnp.where(slot_id < valid, block, gain_rows).astype(BF16)
+    raw[...] = block
+    squares = block * block
+    partial = squares[:, 0:128]
+    for i in range(1, half_s // 128):
+        partial = partial + squares[:, i * 128:(i + 1) * 128]
+    sums = jnp.sum(jnp.transpose(partial), axis=0, keepdims=True)
+    sums = jnp.concatenate([sums, jnp.zeros((1, half_s - slots), F32)], axis=1)
+    hi = sums.astype(BF16).astype(F32)
+    mid = (sums - hi).astype(BF16).astype(F32)
+    lo = sums - hi - mid
+    sum_rows = jnp.where(
+        slot_id == valid, hi, jnp.where(slot_id == valid + 1, mid, jnp.where(slot_id == valid + 2, lo, 0.0))
+    )
+    s_blk[k] = jnp.where(slot_id < valid, block * own_gain, sum_rows).astype(BF16)
     share(s_blk, s2s, s2r)
     s_acc[...] = jnp.zeros_like(s_acc)
     t_acc[...] = jnp.zeros_like(t_acc)
-    sq[...] = jnp.zeros_like(sq)
 
     def student_block(at):
-        x = s_blk[at].astype(F32)
-        scale = jnp.sum(x[valid:], axis=0, keepdims=True)
-        x = jnp.where(slot_id < valid, x, 0.0)
-        squares = x * x
-        partial = squares[:, 0:128]
-        for i in range(1, half_s // 128):
-            partial = partial + squares[:, i * 128:(i + 1) * 128]
-        sq[...] += partial
-        scaled = x * scale
-        hg[at] = jnp.transpose(scaled).astype(BF16)
-        s_acc[...] += jnp.dot(scaled.astype(BF16), wv[at], preferred_element_type=F32)
+        s_acc[...] += jnp.dot(s_blk[at], wv[at], preferred_element_type=F32)
 
     def teacher_block(at):
         t_acc[...] += jnp.dot(t_blk[at], tv[at], preferred_element_type=F32)
@@ -245,6 +241,12 @@
     to_sibling(t_blk, t2s, t2r, 2)
     sibling(s_blk, s2s, s2r, 3)
     student_block(slot(3, 1))
+    sums = s_blk[0][:, 0:slots].astype(F32)[valid:]
+    for i in range(1, 8):
+        sums = sums + s_blk[i][:, 0:slots].astype(F32)[valid:]
+    sums = lax.rsqrt(jnp.sum(sums, axis=0, keepdims=True) / DS + EPSILON)
+    inv = jnp.transpose(jnp.broadcast_to(sums, (slots, slots)))[:, 0:1]
+    live = weight > 0.0
     teacher_block(slot(1, 0))
     teacher_block(slot(2, 0))
     for vm in (1, 2):
@@ -255,7 +257,6 @@
     sibling(t_blk, t2s, t2r, 3)
     teacher_block(slot(3, 1))
 
-    inv = lax.rsqrt(jnp.sum(sq[...], axis=1, keepdims=True) / DS + EPSILON)
     s_log = s_acc[...] * inv
     t_log = t_acc[...]
     top = jnp.max(s_log, axis=1, keepdims=True)
@@ -277,11 +278,15 @@
     st_a[k] = jnp.transpose(packed)[0:8, :]
     for m in range(1, 8):
         send(st_a.at[k], st_a.at[k], as_.at[m], ar.at[m], plane(m // 2, m % 2))
+    for i in range(4):
+        hg[i] = jnp.transpose(s_blk[i].astype(F32)).astype(BF16)
     for m in range(1, 8):
         arrived(st_a.at[slot(m // 2, m % 2)], as_.at[m], ar.at[m], plane(m // 2, m % 2))
     st_b[z] = merge([st_a[i] for i in range(8)])
     for m in range(1, 4):
         send(st_b.at[z], st_b.at[z], bs.at[m], br.at[m], column(m, 0))
+    for i in range(4, 8):
+        hg[i] = jnp.transpose(s_blk[i].astype(F32)).astype(BF16)
     for m in range(1, 4):
         arrived(st_b.at[flip(z, m)], bs.at[m], br.at[m], column(m, 0))
     full = merge([st_b[i] for i in range(4)])
@@ -295,8 +300,8 @@
     back = jnp.concatenate([lse, offset, divergence, cov, jnp.zeros((slots - 4, slots), F32)], axis=0)
     back = jnp.transpose(back)
     prob = jnp.exp(s_log - back[:, 0:1])
-    grad = ((weight * inv) * prob * (s_log - t_log - back[:, 1:2])).astype(BF16)
-    g2[...] = grad
+    grad = (weight * inv) * prob * (s_log - t_log - back[:, 1:2])
+    g2[...] = jnp.where(live, grad, 0.0).astype(BF16)
 
     def block_grad(at):
         return lax.dot_general(g2[...], wv[at], (((1,), (1,)), ((), ())), preferred_element_type=F32)
@@ -318,9 +323,9 @@
     for vm in (1, 2, 3):
         send(p_x.at[vm, :, part:], r_x.at[vm, :, part:], xs.at[vm + 4], xr.at[vm + 4], plane(vm, 0))
 
-    loss_ref[...] = jnp.sum(weight * back[:, 2:3], axis=0, keepdims=True)
+    loss_ref[...] = jnp.sum(jnp.where(live, weight * back[:, 2:3], 0.0), axis=0, keepdims=True)
     lane = lax.broadcasted_iota(jnp.int32, (slots, 128), 1)
-    figure = weight * inv * inv * back[:, 3:4] / DS
+    figure = jnp.where(live, weight * inv * inv * back[:, 3:4] / DS, 0.0)
     hi = figure.astype(BF16).astype(F32)
     mid = (figure - hi).astype(BF16).astype(F32)
     lo = figure - hi - mid
@@ -355,7 +360,7 @@
                 column(m // 2, m % 2),
             )
         gp[:, at] = jnp.sum(
-            total * jnp.where(slot_id < valid, s_blk[k].astype(F32), 0.0)[:, at], axis=0, keepdims=True
+            total * raw[:, at], axis=0, keepdims=True
         )
         if h:
             for m in range(1, 8):
@@ -390,20 +395,13 @@
         copy.wait_send()
 
 
-def finish(
-    head_in, loss_in, hidden_in, gain_in, head_out, loss_out, hidden_out, gain_out,
-    head, hidden, gain, loss, in_sem, out_sem,
-):
-    moves = [(head_in.at[i], head.at[i], head_out.at[i]) for i in range(8)]
-    moves += [(hidden_in, hidden, hidden_out), (gain_in, gain, gain_out), (loss_in, loss, loss_out)]
-    inward = [pltpu.make_async_copy(a, b, in_sem.at[i]) for i, (a, b, _) in enumerate(moves)]
-    outward = [pltpu.make_async_copy(b, c, out_sem.at[i]) for i, (_, b, c) in enumerate(moves)]
-    for copy in inward:
+def finish(head_in, loss_in, hidden_in, gain_in, head_out, loss_out, hidden_out, gain_out, sems):
+    moves = [(head_in.at[i], head_out.at[i]) for i in range(8)]
+    moves += [(hidden_in, hidden_out), (gain_in, gain_out), (loss_in, loss_out)]
+    copies = [pltpu.make_async_copy(src, dst, sems.at[i]) for i, (src, dst) in enumerate(moves)]
+    for copy in copies:
         copy.start()
-    for first, second in zip(inward, outward):
-        first.wait()
-        second.start()
-    for copy in outward:
+    for copy in copies:
         copy.wait()
 
 
@@ -444,7 +442,7 @@
             pltpu.VMEM((8, half_s, slots), BF16),
             pltpu.VMEM((slots, voc), F32),
             pltpu.VMEM((slots, voc), F32),
-            pltpu.VMEM((slots, 128), F32),
+            pltpu.VMEM((slots, half_s), F32),
             pltpu.VMEM((tokens, 128), F32),
             pltpu.VMEM((8, 8, slots), F32),
             pltpu.VMEM((4, 8, slots), F32),
@@ -476,13 +474,7 @@
         out_shape=tuple(jax.ShapeDtypeStruct(r.shape, r.dtype) for r in results),
         in_specs=[hbm] * 4,
         out_specs=(hbm,) * 4,
-        scratch_shapes=[
-            pltpu.VMEM((8, half_s, voc), BF16),
-            pltpu.VMEM((rows, wide_s), BF16),
-            pltpu.VMEM((1, wide_s), F32),
-            pltpu.VMEM((1, 1), F32),
-            dma((11,)), dma((11,)),
-        ],
+        scratch_shapes=[dma((11,))],
         compiler_params=pltpu.CompilerParams(vmem_limit_bytes=LIMIT * 1024),
         cost_estimate=pl.CostEstimate(flops=0, bytes_accessed=6400000, transcendentals=0),
     )(*results)

time: 54.8 us -> 150 us (2.74)
  Pallas kernels: 54 us -> 149 us
    pallas_call x1, Pallas kernels: 3.52 us -> 98.8 us  [fused(): pl.pallas_call(finish, out_shape=tuple((jax.ShapeDtypeStruct(r.shape, r.d...]
where the time goes in v5:
time: 150 us
  Pallas kernels  149 us (99%)
    pallas_call x1, Pallas kernels, fused(): pl.pallas_call(finish, out_shape=tuple((jax.ShapeDtypeStruct(r.shape, r.d...  98.8 us
    pallas_call x1, Pallas kernels, fused(): pl.pallas_call(kernel, out_shape=(jax.ShapeDtypeStruct((1, 1), F32), jax....  50.5 us

profile of v5, /device:TPU:0, one launch (start us, length us, event | category | flops | bytes accessed | tf_op | source)
XLA Modules:
  0.0 149.9 jit_solution(8069984109056306833)
XLA Ops:
  0.6 50.5 %shard_map.102 = (f32[1,1]{1,0:T(1,128)}, bf16[24,1024]{1,0:T(8,128)(2,1)}, f32[1,1024]{1,0:T(1,128)}, bf16[8,512,384]{2,1,0:T(8,128)(2,1)}) custom-call(bf16[24,1024]{1,0:T(8,128)(2,1)} %sh_hbm.1, bf16[24,1280]{1,0:T(8,128)(2,1)} %th_hbm.1, f32[1,1024]{1,0:T(1,128)} %bitcast.11, s32[1,96]{1,0:T(1,128)} %bitcast.13, s32[1,96]{1,0:T(1,128)} %bitcast.14, ...), custom_call_target="tpu_custom_call" | custom-call | flops 2600000000 | bytes 11000000 | tf_op jit(solution)/shard_map/pallas_call | solution.py:420
  51.2 98.8 %shard_map.103 = (bf16[8,512,384]{2,1,0:T(8,128)(2,1)}, f32[1,1]{1,0:T(1,128)}, bf16[24,1024]{1,0:T(8,128)(2,1)}, f32[1,1024]{1,0:T(1,128)}) custom-call(bf16[8,512,384]{2,1,0:T(8,128)(2,1)} %get-tuple-element.12.head_in, f32[1,1]{1,0:T(1,128)} %get-tuple-element.13.loss_in, bf16[24,1024]{1,0:T(8,128)(2,1)} %get-tuple-element.14.hidden_in, ...), custom_call_target="tpu_custom_call" | custom-call | bytes 6400000 | tf_op jit(solution)/shard_map/pallas_call | solution.py:472

commit v6 on v5

--- a/solution.py
+++ b/solution.py
@@ -50,10 +50,10 @@
 def kernel(
     sh_hbm, th_hbm, gain_hbm, source_hbm, lengths_hbm, w_hbm, t_hbm,
     loss_ref, gh_ref, gg_ref, head_hbm,
-    wv, tv, sh_ref, gain_ref, source_ref, lengths_ref, pick_ref, in_s, in_t, s_blk, t_blk, hg, s_acc, t_acc, raw, cols,
+    wv, tv, sh_ref, gain_ref, source_ref, lengths_ref, pick_ref, in_s, in_t, s_blk, t_blk, hg, s_acc, t_acc, raw, sq, cols,
     st_a, st_b, g2, own, p_sib, r_sib, p_x, r_x, rb, rz, gp, gz, head,
     w_sem, t_sem, h_sem, l_sem, s1s, s1r, t1s, t1r, s2s, s2r, t2s, t2r, as_, ar, bs, br,
-    qs, qr, xs, xr, zs, zr, ys, yr,
+    qs, qr, xs, xr, zs, zr, ys, yr, us, ur,
 ):
     g = lax.axis_index("grp")
     v = lax.axis_index("voc")
@@ -62,7 +62,6 @@
     rows, half_s = in_s.shape[1], in_s.shape[2]
     half_t = in_t.shape[2]
     tokens = in_s.shape[0] * rows
-    valid = tokens * 5 // 8
     slots = s_acc.shape[0]
 
     def plane(vm, cm):
@@ -111,12 +110,40 @@
         pl.semaphore_signal(barrier, inc=1, device_id=peer, device_id_type=MESH)
     pl.semaphore_wait(barrier, len(peers))
 
-    for m in range(1, 8):
-        other = 1 - c if m % 2 else c
-        send(half(sh_hbm, other, half_s), in_s.at[g], s1s.at[m], s1r.at[m], column(m // 2, m % 2))
-    for m in range(1, 8):
-        other = 1 - c if m % 2 else c
-        send(half(th_hbm, other, half_t), in_t.at[g], t1s.at[m], t1r.at[m], column(m // 2, m % 2))
+    def source(m):
+        return flip(z, m // 2) * 2 + (1 - c if m % 2 else c)
+
+    middle = (z == 1) | (z == 2)
+    middle_sends = []
+
+    def spread_rows(ref, width, dst, ssem, rsem):
+        for m in (4, 5, 6, 7, 2, 3, 1):
+            other = 1 - c if m % 2 else c
+            if m < 6:
+                send(half(ref, other, width), dst.at[g], ssem.at[m], rsem.at[m], column(m // 2, m % 2))
+            else:
+                middle_sends.append(pltpu.make_async_remote_copy(
+                    src_ref=half(ref, other, width), dst_ref=dst.at[g], send_sem=ssem.at[m], recv_sem=rsem.at[m],
+                    device_id=column(m // 2, m % 2), device_id_type=MESH,
+                ))
+                pl.when(middle)(middle_sends[-1].start)
+
+    def hand_on(dst, ssem, rsem):
+        for m in (4, 5):
+            piece = dst.at[source(m)]
+            arrived(piece, ssem.at[m], rsem.at[m], column(2, m % 2))
+            middle_sends.append(pltpu.make_async_remote_copy(
+                src_ref=piece, dst_ref=piece, send_sem=ssem.at[m + 4], recv_sem=rsem.at[m + 2],
+                device_id=column(1, 0), device_id_type=MESH,
+            ))
+            pl.when(middle)(middle_sends[-1].start)
+
+    def rows_in(dst, ssem, rsem):
+        for m in (1, 2, 3, 6, 7):
+            arrived(dst.at[source(m)], ssem.at[m], rsem.at[m], column(m // 2, m % 2))
+
+    spread_rows(sh_hbm, half_s, in_s, s1s, s1r)
+    spread_rows(th_hbm, half_t, in_t, t1s, t1r)
 
     for copy in local_copies[:3]:
         copy.wait()
@@ -149,10 +176,6 @@
 
     gain = gain_ref[...]
     own_gain = jnp.where(c == 0, gain[:, :half_s], gain[:, half_s:])
-    slot_id = lax.broadcasted_iota(jnp.int32, (slots, half_s), 0)
-
-    def source(m):
-        return flip(z, m // 2) * 2 + (1 - c if m % 2 else c)
 
     halves = (slice(0, slots // 2), slice(slots // 2, slots))
 
@@ -181,27 +204,22 @@
     def sibling(blk, ssem, rsem, vm):
         arrived(blk.at[slot(vm, 1)], ssem.at[vm * 4 + 2], rsem.at[vm * 4 + 2], plane(0, 1))
 
-    for m in range(1, 8):
-        arrived(in_s.at[source(m)], s1s.at[m], s1r.at[m], column(m // 2, m % 2))
+    hand_on(in_s, s1s, s1r)
+    rows_in(in_s, s1s, s1r)
     for copy in local_copies[3:]:
         copy.wait()
     block = jnp.concatenate([in_s[i].astype(F32) for i in range(8)], axis=0).astype(BF16)
     block = jnp.dot(pick, block, preferred_element_type=F32)
     raw[...] = block
+    s_blk[k] = (block * own_gain).astype(BF16)
+    share(s_blk, s2s, s2r)
     squares = block * block
     partial = squares[:, 0:128]
     for i in range(1, half_s // 128):
         partial = partial + squares[:, i * 128:(i + 1) * 128]
-    sums = jnp.sum(jnp.transpose(partial), axis=0, keepdims=True)
-    sums = jnp.concatenate([sums, jnp.zeros((1, half_s - slots), F32)], axis=1)
-    hi = sums.astype(BF16).astype(F32)
-    mid = (sums - hi).astype(BF16).astype(F32)
-    lo = sums - hi - mid
-    sum_rows = jnp.where(
-        slot_id == valid, hi, jnp.where(slot_id == valid + 1, mid, jnp.where(slot_id == valid + 2, lo, 0.0))
-    )
-    s_blk[k] = jnp.where(slot_id < valid, block * own_gain, sum_rows).astype(BF16)
-    share(s_blk, s2s, s2r)
+    sq[k] = jnp.broadcast_to(jnp.sum(jnp.transpose(partial), axis=0, keepdims=True), (8, slots))
+    for m in range(1, 8):
+        send(sq.at[k], sq.at[k], us.at[m], ur.at[m], plane(m // 2, m % 2))
     s_acc[...] = jnp.zeros_like(s_acc)
     t_acc[...] = jnp.zeros_like(t_acc)
 
@@ -213,11 +231,11 @@
 
     w_copy.wait()
     student_block(k)
+    hand_on(in_t, t1s, t1r)
     sibling(s_blk, s2s, s2r, 0)
     student_block(slot(0, 1))
     relay(s_blk, s2s, s2r)
-    for m in range(1, 8):
-        arrived(in_t.at[source(m)], t1s.at[m], t1r.at[m], column(m // 2, m % 2))
+    rows_in(in_t, t1s, t1r)
     block = jnp.concatenate([in_t[i].astype(F32) for i in range(8)], axis=0).astype(BF16)
     t_blk[k] = jnp.dot(pick_t, block, preferred_element_type=F32).astype(BF16)
     share(t_blk, t2s, t2r)
@@ -241,10 +259,12 @@
     to_sibling(t_blk, t2s, t2r, 2)
     sibling(s_blk, s2s, s2r, 3)
     student_block(slot(3, 1))
-    sums = s_blk[0][:, 0:slots].astype(F32)[valid:]
+    for m in range(1, 8):
+        arrived(sq.at[slot(m // 2, m % 2)], us.at[m], ur.at[m], plane(m // 2, m % 2))
+    sums = sq[0, 0:1]
     for i in range(1, 8):
-        sums = sums + s_blk[i][:, 0:slots].astype(F32)[valid:]
-    sums = lax.rsqrt(jnp.sum(sums, axis=0, keepdims=True) / DS + EPSILON)
+        sums = sums + sq[i, 0:1]
+    sums = lax.rsqrt(sums / DS + EPSILON)
     inv = jnp.transpose(jnp.broadcast_to(sums, (slots, slots)))[:, 0:1]
     live = weight > 0.0
     teacher_block(slot(1, 0))
@@ -393,15 +413,24 @@
         copy.wait()
     for copy in sends:
         copy.wait_send()
-
-
-def finish(head_in, loss_in, hidden_in, gain_in, head_out, loss_out, hidden_out, gain_out, sems):
-    moves = [(head_in.at[i], head_out.at[i]) for i in range(8)]
-    moves += [(hidden_in, hidden_out), (gain_in, gain_out), (loss_in, loss_out)]
-    copies = [pltpu.make_async_copy(src, dst, sems.at[i]) for i, (src, dst) in enumerate(moves)]
-    for copy in copies:
+    for copy in middle_sends:
+        pl.when(middle)(copy.wait_send)
+
+
+def finish(
+    head_in, loss_in, hidden_in, gain_in, head_out, loss_out, hidden_out, gain_out,
+    head, hidden, gain, loss, in_sem, out_sem,
+):
+    moves = [(head_in.at[i], head.at[i], head_out.at[i]) for i in range(8)]
+    moves += [(hidden_in, hidden, hidden_out), (gain_in, gain, gain_out), (loss_in, loss, loss_out)]
+    inward = [pltpu.make_async_copy(a, b, in_sem.at[i]) for i, (a, b, _) in enumerate(moves)]
+    outward = [pltpu.make_async_copy(b, c, out_sem.at[i]) for i, (_, b, c) in enumerate(moves)]
+    for copy in inward:
         copy.start()
-    for copy in copies:
+    for first, second in zip(inward, outward):
+        first.wait()
+        second.start()
+    for copy in outward:
         copy.wait()
 
 
@@ -413,7 +442,7 @@
     tokens = rows * lax.axis_size("grp")
     voc = student_head.shape[1]
     half_s, half_t = wide_s // 2, wide_t // 2
-    slots = -(-(tokens * 5 // 8 + 3) // 128) * 128
+    slots = -(-(tokens * 5 // 8) // 128) * 128
     vmem = pl.BlockSpec(memory_space=pltpu.VMEM)
     hbm = pl.BlockSpec(memory_space=pltpu.HBM)
     dma = pltpu.SemaphoreType.DMA
@@ -443,6 +472,7 @@
             pltpu.VMEM((slots, voc), F32),
             pltpu.VMEM((slots, voc), F32),
             pltpu.VMEM((slots, half_s), F32),
+            pltpu.VMEM((8, 8, slots), F32),
             pltpu.VMEM((tokens, 128), F32),
             pltpu.VMEM((8, 8, slots), F32),
             pltpu.VMEM((4, 8, slots), F32),
@@ -458,7 +488,7 @@
             pltpu.VMEM((8, 1, half_s), F32),
             pltpu.VMEM((8, half_s, voc), BF16),
             dma(()), dma(()), dma((8,)), dma((8,)),
-        ] + [dma((8,))] * 4 + [dma((16,))] * 4 + [dma((8,))] * 8 + [dma((16,))] * 2 + [dma((8,))] * 2,
+        ] + [dma((16,))] * 8 + [dma((8,))] * 8 + [dma((16,))] * 2 + [dma((8,))] * 4,
         compiler_params=pltpu.CompilerParams(
             collective_id=0, has_side_effects=True, vmem_limit_bytes=LIMIT * 1024
         ),
@@ -474,7 +504,13 @@
         out_shape=tuple(jax.ShapeDtypeStruct(r.shape, r.dtype) for r in results),
         in_specs=[hbm] * 4,
         out_specs=(hbm,) * 4,
-        scratch_shapes=[dma((11,))],
+        scratch_shapes=[
+            pltpu.VMEM((8, half_s, voc), BF16),
+            pltpu.VMEM((rows, wide_s), BF16),
+            pltpu.VMEM((1, wide_s), F32),
+            pltpu.VMEM((1, 1), F32),
+            dma((11,)), dma((11,)),
+        ],
         compiler_params=pltpu.CompilerParams(vmem_limit_bytes=LIMIT * 1024),
         cost_estimate=pl.CostEstimate(flops=0, bytes_accessed=6400000, transcendentals=0),
     )(*results)

time: 150 us -> 55.8 us (0.37)
  Pallas kernels: 149 us -> 55 us
    pallas_call x1, Pallas kernels: 98.8 us -> 3.52 us  [fused(): pl.pallas_call(finish, out_shape=tuple((jax.ShapeDtypeStruct(r.shape, r.d...]
where the time goes in v6:
time: 55.8 us; the launch traced here: 55.6 us
  Pallas kernels  55 us (99%)
  between operations  0.64 us (1%)
    pallas_call x1, Pallas kernels, fused(): pl.pallas_call(kernel, out_shape=(jax.ShapeDtypeStruct((1, 1), F32), jax....  51.5 us
    pallas_call x1, Pallas kernels, fused(): pl.pallas_call(finish, out_shape=tuple((jax.ShapeDtypeStruct(r.shape, r.d...  3.52 us

profile of v6, /device:TPU:0, one launch (start us, length us, event | category | flops | bytes accessed | tf_op | source)
XLA Modules:
  0.0 55.6 jit_solution(3284632768904636765)
XLA Ops:
  0.6 51.5 %shard_map.102 = (f32[1,1]{1,0:T(1,128)}, bf16[24,1024]{1,0:T(8,128)(2,1)}, f32[1,1024]{1,0:T(1,128)}, bf16[8,512,384]{2,1,0:T(8,128)(2,1)}) custom-call(bf16[24,1024]{1,0:T(8,128)(2,1)} %sh_hbm.1, bf16[24,1280]{1,0:T(8,128)(2,1)} %th_hbm.1, f32[1,1024]{1,0:T(1,128)} %bitcast.11, s32[1,96]{1,0:T(1,128)} %bitcast.13, s32[1,96]{1,0:T(1,128)} %bitcast.14, ...), custom_call_target="tpu_custom_call" | custom-call | flops 2600000000 | bytes 11000000 | tf_op jit(solution)/shard_map/pallas_call | solution.py:449
  52.1 3.5 %shard_map.103 = (bf16[8,512,384]{2,1,0:T(8,128)(2,1)}, f32[1,1]{1,0:T(1,128)}, bf16[24,1024]{1,0:T(8,128)(2,1)}, f32[1,1024]{1,0:T(1,128)}) custom-call(bf16[8,512,384]{2,1,0:T(8,128)(2,1)} %get-tuple-element.12.head_in, f32[1,1]{1,0:T(1,128)} %get-tuple-element.13.loss_in, bf16[24,1024]{1,0:T(8,128)(2,1)} %get-tuple-element.14.hidden_in, ...), custom_call_target="tpu_custom_call" | custom-call | bytes 6400000 | tf_op jit(solution)/shard_map/pallas_call | solution.py:502

commit v7 on v6

--- a/solution.py
+++ b/solution.py
@@ -113,33 +113,13 @@
     def source(m):
         return flip(z, m // 2) * 2 + (1 - c if m % 2 else c)
 
-    middle = (z == 1) | (z == 2)
-    middle_sends = []
-
     def spread_rows(ref, width, dst, ssem, rsem):
-        for m in (4, 5, 6, 7, 2, 3, 1):
+        for m in (6, 7, 4, 5, 2, 3, 1):
             other = 1 - c if m % 2 else c
-            if m < 6:
-                send(half(ref, other, width), dst.at[g], ssem.at[m], rsem.at[m], column(m // 2, m % 2))
-            else:
-                middle_sends.append(pltpu.make_async_remote_copy(
-                    src_ref=half(ref, other, width), dst_ref=dst.at[g], send_sem=ssem.at[m], recv_sem=rsem.at[m],
-                    device_id=column(m // 2, m % 2), device_id_type=MESH,
-                ))
-                pl.when(middle)(middle_sends[-1].start)
-
-    def hand_on(dst, ssem, rsem):
-        for m in (4, 5):
-            piece = dst.at[source(m)]
-            arrived(piece, ssem.at[m], rsem.at[m], column(2, m % 2))
-            middle_sends.append(pltpu.make_async_remote_copy(
-                src_ref=piece, dst_ref=piece, send_sem=ssem.at[m + 4], recv_sem=rsem.at[m + 2],
-                device_id=column(1, 0), device_id_type=MESH,
-            ))
-            pl.when(middle)(middle_sends[-1].start)
+            send(half(ref, other, width), dst.at[g], ssem.at[m], rsem.at[m], column(m // 2, m % 2))
 
     def rows_in(dst, ssem, rsem):
-        for m in (1, 2, 3, 6, 7):
+        for m in range(1, 8):
             arrived(dst.at[source(m)], ssem.at[m], rsem.at[m], column(m // 2, m % 2))
 
     spread_rows(sh_hbm, half_s, in_s, s1s, s1r)
@@ -204,7 +184,6 @@
     def sibling(blk, ssem, rsem, vm):
         arrived(blk.at[slot(vm, 1)], ssem.at[vm * 4 + 2], rsem.at[vm * 4 + 2], plane(0, 1))
 
-    hand_on(in_s, s1s, s1r)
     rows_in(in_s, s1s, s1r)
     for copy in local_copies[3:]:
         copy.wait()
@@ -231,7 +210,6 @@
 
     w_copy.wait()
     student_block(k)
-    hand_on(in_t, t1s, t1r)
     sibling(s_blk, s2s, s2r, 0)
     student_block(slot(0, 1))
     relay(s_blk, s2s, s2r)
@@ -326,7 +304,7 @@
     def block_grad(at):
         return lax.dot_general(g2[...], wv[at], (((1,), (1,)), ((), ())), preferred_element_type=F32)
 
-    order = (1, 2, 3, 0)
+    order = (3, 1, 2, 0)
     part = half_s // 2
     for vm in order:
         p_sib[vm] = block_grad(slot(vm, 1)).astype(BF16)
@@ -340,7 +318,7 @@
             send(p_x.at[vm, :, 0:part], r_x.at[vm, :, 0:part], xs.at[vm], xr.at[vm], plane(vm, 0))
         else:
             own[...] = mine
-    for vm in (1, 2, 3):
+    for vm in (3, 1, 2):
         send(p_x.at[vm, :, part:], r_x.at[vm, :, part:], xs.at[vm + 4], xr.at[vm + 4], plane(vm, 0))
 
     loss_ref[...] = jnp.sum(jnp.where(live, weight * back[:, 2:3], 0.0), axis=0, keepdims=True)
@@ -413,8 +391,6 @@
         copy.wait()
     for copy in sends:
         copy.wait_send()
-    for copy in middle_sends:
-        pl.when(middle)(copy.wait_send)
 
 
 def finish(

time: 55.8 us -> 57.7 us (1.034)
  Pallas kernels: 55 us -> 56.9 us
    pallas_call x1, Pallas kernels: 51.5 us -> 53.4 us  [fused(): pl.pallas_call(kernel, out_shape=(jax.ShapeDtypeStruct((1, 1), F32), jax....]
where the time goes in v7:
time: 57.7 us; the launch traced here: 57.5 us
  Pallas kernels  56.9 us (99%)
  between operations  0.64 us (1%)
    pallas_call x1, Pallas kernels, fused(): pl.pallas_call(kernel, out_shape=(jax.ShapeDtypeStruct((1, 1), F32), jax....  53.4 us
    pallas_call x1, Pallas kernels, fused(): pl.pallas_call(finish, out_shape=tuple((jax.ShapeDtypeStruct(r.shape, r.d...  3.52 us

profile of v7, /device:TPU:0, one launch (start us, length us, event | category | flops | bytes accessed | tf_op | source)
XLA Modules:
  0.0 57.5 jit_solution(13198601650121447843)
XLA Ops:
  0.6 53.4 %shard_map.102 = (f32[1,1]{1,0:T(1,128)}, bf16[24,1024]{1,0:T(8,128)(2,1)}, f32[1,1024]{1,0:T(1,128)}, bf16[8,512,384]{2,1,0:T(8,128)(2,1)}) custom-call(bf16[24,1024]{1,0:T(8,128)(2,1)} %sh_hbm.1, bf16[24,1280]{1,0:T(8,128)(2,1)} %th_hbm.1, f32[1,1024]{1,0:T(1,128)} %bitcast.11, s32[1,96]{1,0:T(1,128)} %bitcast.13, s32[1,96]{1,0:T(1,128)} %bitcast.14, ...), custom_call_target="tpu_custom_call" | custom-call | flops 2600000000 | bytes 11000000 | tf_op jit(solution)/shard_map/pallas_call | solution.py:425
  54.0 3.5 %shard_map.103 = (bf16[8,512,384]{2,1,0:T(8,128)(2,1)}, f32[1,1]{1,0:T(1,128)}, bf16[24,1024]{1,0:T(8,128)(2,1)}, f32[1,1024]{1,0:T(1,128)}) custom-call(bf16[8,512,384]{2,1,0:T(8,128)(2,1)} %get-tuple-element.12.head_in, f32[1,1]{1,0:T(1,128)} %get-tuple-element.13.loss_in, bf16[24,1024]{1,0:T(8,128)(2,1)} %get-tuple-element.14.hidden_in, ...), custom_call_target="tpu_custom_call" | custom-call | bytes 6400000 | tf_op jit(solution)/shard_map/pallas_call | solution.py:478

commit v8 on v6

--- a/solution.py
+++ b/solution.py
@@ -117,7 +117,7 @@
     middle_sends = []
 
     def spread_rows(ref, width, dst, ssem, rsem):
-        for m in (4, 5, 6, 7, 2, 3, 1):
+        for m in range(1, 8):
             other = 1 - c if m % 2 else c
             if m < 6:
                 send(half(ref, other, width), dst.at[g], ssem.at[m], rsem.at[m], column(m // 2, m % 2))

time: 55.8 us -> 56.3 us (level)
  no operation moved by 1% of the time
where the time goes in v8:
time: 56.3 us; the launch traced here: 56.2 us
  Pallas kernels  55.5 us (99%)
  between operations  0.64 us (1%)
    pallas_call x1, Pallas kernels, fused(): pl.pallas_call(kernel, out_shape=(jax.ShapeDtypeStruct((1, 1), F32), jax....  52 us
    pallas_call x1, Pallas kernels, fused(): pl.pallas_call(finish, out_shape=tuple((jax.ShapeDtypeStruct(r.shape, r.d...  3.52 us

profile of v8, /device:TPU:0, one launch (start us, length us, event | category | flops | bytes accessed | tf_op | source)
XLA Modules:
  0.0 56.2 jit_solution(13500225252901951076)
XLA Ops:
  0.6 52.0 %shard_map.102 = (f32[1,1]{1,0:T(1,128)}, bf16[24,1024]{1,0:T(8,128)(2,1)}, f32[1,1024]{1,0:T(1,128)}, bf16[8,512,384]{2,1,0:T(8,128)(2,1)}) custom-call(bf16[24,1024]{1,0:T(8,128)(2,1)} %sh_hbm.1, bf16[24,1280]{1,0:T(8,128)(2,1)} %th_hbm.1, f32[1,1024]{1,0:T(1,128)} %bitcast.11, s32[1,96]{1,0:T(1,128)} %bitcast.13, s32[1,96]{1,0:T(1,128)} %bitcast.14, ...), custom_call_target="tpu_custom_call" | custom-call | flops 2600000000 | bytes 11000000 | tf_op jit(solution)/shard_map/pallas_call | solution.py:449
  52.7 3.5 %shard_map.103 = (bf16[8,512,384]{2,1,0:T(8,128)(2,1)}, f32[1,1]{1,0:T(1,128)}, bf16[24,1024]{1,0:T(8,128)(2,1)}, f32[1,1024]{1,0:T(1,128)}) custom-call(bf16[8,512,384]{2,1,0:T(8,128)(2,1)} %get-tuple-element.12.head_in, f32[1,1]{1,0:T(1,128)} %get-tuple-element.13.loss_in, bf16[24,1024]{1,0:T(8,128)(2,1)} %get-tuple-element.14.hidden_in, ...), custom_call_target="tpu_custom_call" | custom-call | bytes 6400000 | tf_op jit(solution)/shard_map/pallas_call | solution.py:502
